TPU v7x, 256 devices: a whole 4x4x8 slice. The times are simulated.
256 devices in a mesh: member: 2 (over core), node: 32 (over z, x), tensor: 4 (over y).
Axes of the slice: x: 4, y: 4, z: 8, core: 2. Of those that a mesh axis runs over, the one named last changes fastest.
Arguments:
- layer_in: bfloat16 [131072, 512], P(('member', 'node', 'tensor')), parts along dimension 0, may hold values from -6 to 6
- output_gradient: bfloat16 [131072, 512], P(('member', 'node', 'tensor')), parts along dimension 0, may hold values from -6 to 6
- attention_gain: float32 [512], replicated, may hold values from 0.5 to 1.5
- feedforward_gain: float32 [512], replicated, may hold values from 0.5 to 1.5
- w_query: bfloat16 [512, 512], replicated, may hold values from -1.3258252 to 1.3258252
- w_key: bfloat16 [512, 512], replicated, may hold values from -1.41421356 to 1.41421356
- w_value: bfloat16 [512, 512], replicated, may hold values from -0.25 to 0.25
- w_out: bfloat16 [512, 512], replicated, may hold values from -0.25 to 0.25
- w_up: bfloat16 [512, 2048], P(None, 'tensor'), may hold values from -0.25 to 0.25
- w_down: bfloat16 [2048, 512], P('tensor'), may hold values from -0.125 to 0.125
- neighbours: int32 [512, 8], P(('node', 'tensor')), may hold values from 0 to 511, as said below
- counts: int32 [512], P(('node', 'tensor')), may hold values from 3 to 8, as said below
- node_mask: int32 [512, 128], replicated, may hold values from 0 to 1, as said below
Outputs:
- grad_in: bfloat16 [131072, 512], P(('member', 'node', 'tensor')), parts along dimension 0
There are 2 independent parts, one for each index of `member`. A program takes and returns all parts, laid end to end along the dimension named above; an argument that names none is the same for every part. Nothing has to cross between parts.
Inputs may be any that keep to these rules, and one draw needn't show every extreme that they name: `neighbours`: slot 0 of row b is b itself; slots below counts[b] hold distinct blocks whose index differs from b by at most 4; slots from counts[b] on hold b and are ignored. `counts`: 8 is reached in every draw. `node_mask`: in each block the live nodes come first, at least 64 of them.
All inputs are finite; a program needn't handle non-finite values.
Results may differ from a plain program's by a relative error of at most 0.015.
The roundings to bfloat16 on the way count: a program that leaves them out, or rounds other values in their place, can miss the bound.
Values may be sent and summed in bfloat16 or wider, within the bound.
A program may use at most 256 MiB of HBM per device.

v0:
```python
import jax
import jax.numpy as jnp
from jax import lax
from jax.sharding import PartitionSpec as P

HEADS = 8
HEAD_DIM = 64
NBR = 8
SPAN = 4


NORM_EPS = 1e-05
GELU_C = 0.7978845608028654
GELU_A = 0.044715


def with_halo(block, sides, width):
    for axis, dim in sides:
        count = lax.axis_size(axis)
        forward = [(i, i + 1) for i in range(count - 1)]
        backward = [(target, source) for source, target in forward]
        low = lax.ppermute(
            lax.slice_in_dim(block, block.shape[dim] - width, None, axis=dim), axis, forward
        )
        high = lax.ppermute(lax.slice_in_dim(block, 0, width, axis=dim), axis, backward)
        block = jnp.concatenate([low, block, high], axis=dim)
    return block


def norm_apply_step(values, gain):
    centre = jnp.mean(values, axis=-1, keepdims=True)
    centred = values - centre
    inverse = lax.rsqrt(jnp.mean(centred * centred, axis=-1, keepdims=True) + NORM_EPS)
    normed = centred * inverse
    return ((normed * gain).astype(jnp.bfloat16), normed, inverse)


def norm_reverse_step(upstream, normed, inverse, gain):
    scaled = upstream * gain
    first_mean = jnp.mean(scaled, axis=-1, keepdims=True)
    second_mean = jnp.mean(scaled * normed, axis=-1, keepdims=True)
    return inverse * (scaled - first_mean - normed * second_mean)


def gelu_slope(pre_act):
    inner = GELU_C * (pre_act + GELU_A * pre_act**3)
    tangent = jnp.tanh(inner)
    return 0.5 * (1.0 + tangent) + 0.5 * pre_act * (1.0 - tangent * tangent) * GELU_C * (
        1.0 + 3.0 * GELU_A * pre_act * pre_act
    )


def dot_last(left, right):
    return lax.dot_general(
        left, right, (((1,), (1,)), ((), ())), preferred_element_type=jnp.float32
    )


def head_split(matrix):
    return matrix.reshape(matrix.shape[0], HEADS, HEAD_DIM)


def block_probs(query, key_rows, valid):
    scores = jnp.einsum(
        "qhd,khd->hqk", head_split(query), head_split(key_rows), preferred_element_type=jnp.float32
    ) * HEAD_DIM ** (-0.5)
    scores = jnp.where(valid[None, None, :], scores, -1e30)
    top_score = jnp.max(scores, axis=-1, keepdims=True)
    expo = jnp.exp(scores - top_score)
    total = jnp.sum(expo, axis=-1, keepdims=True)
    return (expo / total, top_score, total)


def key_value_grads(probs, query, upstream, near_values):
    weights = probs.astype(jnp.bfloat16)
    upstream_heads = head_split(upstream)
    grad_prob = jnp.einsum(
        "qhd,khd->hqk", upstream_heads, head_split(near_values), preferred_element_type=jnp.float32
    )
    centre = jnp.sum(probs * grad_prob, axis=-1, keepdims=True)
    grad_score = (probs * (grad_prob - centre) * HEAD_DIM ** (-0.5)).astype(jnp.bfloat16)
    grad_keys = jnp.einsum(
        "hqk,qhd->khd", grad_score, head_split(query), preferred_element_type=jnp.float32
    )
    grad_values = jnp.einsum(
        "hqk,qhd->khd", weights, upstream_heads, preferred_element_type=jnp.float32
    )
    return (grad_score, grad_keys, grad_values, centre)


def body(
    layer_in,
    output_gradient,
    attention_gain,
    feedforward_gain,
    w_query,
    w_key,
    w_value,
    w_out,
    w_up,
    w_down,
    neighbours,
    counts,
    node_mask,
):
    row_count = layer_in.shape[0]
    width = layer_in.shape[1]
    block_count = counts.shape[0]
    block_len = row_count // block_count
    input_float_rows = layer_in.astype(jnp.float32)
    first_normed_rows, first_centred_scaled, first_inverse_norm = norm_apply_step(
        input_float_rows, attention_gain
    )
    queries = jnp.dot(first_normed_rows, w_query, preferred_element_type=jnp.float32).astype(
        jnp.bfloat16
    )
    key_local = jnp.dot(first_normed_rows, w_key, preferred_element_type=jnp.float32).astype(
        jnp.bfloat16
    )
    value_local = jnp.dot(first_normed_rows, w_value, preferred_element_type=jnp.float32).astype(
        jnp.bfloat16
    )
    paired = jnp.stack(
        [
            key_local.reshape(block_count, block_len, width),
            value_local.reshape(block_count, block_len, width),
        ],
        axis=1,
    )
    extended = with_halo(paired, ((("node", "tensor"), 0),), SPAN)
    first_block = lax.axis_index(("node", "tensor")) * block_count - SPAN
    local_ids = neighbours - first_block
    near_all = extended[local_ids]
    slot_ok = jnp.arange(NBR, dtype=jnp.int32)[None, :] < counts[:, None]
    live_keys = (node_mask[neighbours] > 0) & slot_ok[:, :, None]
    query_blocks = queries.reshape(block_count, block_len, width)

    def attend(packed):
        query, near_pair, valid = packed
        near_keys = near_pair[:, 0].reshape(-1, width)
        near_values = near_pair[:, 1].reshape(-1, width)
        weights = block_probs(query, near_keys, valid.reshape(-1))[0].astype(jnp.bfloat16)
        mixed = jnp.einsum(
            "hqk,khd->qhd", weights, head_split(near_values), preferred_element_type=jnp.float32
        )
        return mixed.reshape(block_len, width).astype(jnp.bfloat16)

    attended = lax.map(attend, (query_blocks, near_all, live_keys)).reshape(row_count, width)
    middle_state = input_float_rows + jnp.dot(attended, w_out, preferred_element_type=jnp.float32)
    second_normed_rows, second_centred_scaled, second_inverse_norm = norm_apply_step(
        middle_state, feedforward_gain
    )
    rows_all, upstream_all = (
        lax.all_gather(second_normed_rows, "tensor", axis=0, tiled=True),
        lax.all_gather(output_gradient, "tensor", axis=0, tiled=True),
    )
    pre_act = jnp.dot(rows_all, w_up, preferred_element_type=jnp.float32)
    grad_mid = dot_last(upstream_all, w_down)
    grad_act = (grad_mid * gelu_slope(pre_act)).astype(jnp.bfloat16)
    second_norm_gradient = lax.psum_scatter(
        dot_last(grad_act, w_up), "tensor", scatter_dimension=0, tiled=True
    )
    residual_middle_gradient = output_gradient.astype(jnp.float32) + norm_reverse_step(
        second_norm_gradient, second_centred_scaled, second_inverse_norm, feedforward_gain
    )
    grad_attended = jnp.dot(
        residual_middle_gradient.astype(jnp.bfloat16), w_out.T, preferred_element_type=jnp.float32
    ).astype(jnp.bfloat16)
    grad_blocks = grad_attended.reshape(block_count, block_len, width)

    def backward(packed):
        query, near_pair, valid, upstream = packed
        near_keys = near_pair[:, 0].reshape(-1, width)
        near_values = near_pair[:, 1].reshape(-1, width)
        probs, top_score, total = block_probs(query, near_keys, valid.reshape(-1))
        grad_score, grad_keys, grad_values, centre = key_value_grads(
            probs, query, upstream, near_values
        )
        grad_query = jnp.einsum(
            "hqk,khd->qhd", grad_score, head_split(near_keys), preferred_element_type=jnp.float32
        )
        stacked = jnp.stack(
            [grad_keys.reshape(NBR, block_len, width), grad_values.reshape(NBR, block_len, width)],
            axis=1,
        )
        summary = jnp.stack([(top_score + jnp.log(total))[:, :, 0], centre[:, :, 0]], axis=0)
        return (grad_query.reshape(block_len, width).astype(jnp.bfloat16), stacked, summary)

    grad_query_blocks, neighbour_gradient, summaries = lax.map(
        backward, (query_blocks, near_all, live_keys, grad_blocks)
    )
    slot_index = jnp.arange(block_count + 2 * SPAN, dtype=jnp.int32)
    neighbour_picker = (local_ids[:, :, None] == slot_index[None, None, :]).astype(jnp.float32)
    gradient_sum_rows = jnp.einsum(
        "qix,qigzo->xgzo", neighbour_picker, neighbour_gradient, precision=lax.Precision.HIGHEST
    )
    rims = jnp.concatenate(
        [gradient_sum_rows[:SPAN], gradient_sum_rows[block_count + SPAN :]], axis=0
    )
    returned = with_halo(rims, ((("node", "tensor"), 0),), SPAN)
    from_lower = returned[:SPAN]
    from_upper = returned[3 * SPAN :]
    own_sums = gradient_sum_rows[SPAN : SPAN + block_count] + from_lower + from_upper
    grad_queries = grad_query_blocks.reshape(row_count, width)
    grad_keys_own = own_sums[:, 0].reshape(row_count, width).astype(jnp.bfloat16)
    grad_values_own = own_sums[:, 1].reshape(row_count, width).astype(jnp.bfloat16)
    first_norm_gradient = (
        jnp.dot(grad_queries, w_query.T, preferred_element_type=jnp.float32)
        + jnp.dot(grad_keys_own, w_key.T, preferred_element_type=jnp.float32)
        + jnp.dot(grad_values_own, w_value.T, preferred_element_type=jnp.float32)
    )
    return (
        residual_middle_gradient
        + norm_reverse_step(
            first_norm_gradient, first_centred_scaled, first_inverse_norm, attention_gain
        )
    ).astype(jnp.bfloat16)


def solution(mesh):
    return jax.shard_map(
        body,
        mesh=mesh,
        in_specs=(
            P(("member", "node", "tensor"), None),
            P(("member", "node", "tensor"), None),
            P(),
            P(),
            P(),
            P(),
            P(),
            P(),
            P(None, "tensor"),
            P("tensor", None),
            P(("node", "tensor"), None),
            P(("node", "tensor")),
            P(),
        ),
        out_specs=P(("member", "node", "tensor"), None),
        check_vma=False,
    )
```

profile of v0, /device:TPU:160, one launch (start us, length us, event | category | flops | bytes accessed | tf_op | source)
XLA Modules:
  0.0 528.5 jit_solution(15788658887069928659)
XLA Ops:
  10.6 7.6 %collective-permute-start.1 = (bf16[4,2,128,512]{3,2,0,1:T(8,128)(2,1)S(1)}, bf16[4,2,128,512]{3,2,0,1:T(8,128)(2,1)}, u32[]{:S(2)}, u32[]{:S(2)}) collective-permute-start(bf16[4,2,128,512]{3,2,0,1:T(8,128)(2,1)S(1)} %pad_maximum_fusion.1), channel_id=1, source_target_pairs={{1,0},{2,1},{3,2},{4,3},{5,4},{6,5},{7,6},{8,7},{9,8},{10,9},{11,1... | collective-permute-start | bytes 3145736 | tf_op jit(solution)/shard_map/ppermute | solution.py:25
  26.1 14.5 %collective-permute-done.1 = bf16[4,2,128,512]{3,2,0,1:T(8,128)(2,1)} collective-permute-done((bf16[4,2,128,512]{3,2,0,1:T(8,128)(2,1)S(1)}, bf16[4,2,128,512]{3,2,0,1:T(8,128)(2,1)}, u32[]{:S(2)}, u32[]{:S(2)}) %collective-permute-start.1) | collective-permute-done | bytes 1048608 | tf_op jit(solution)/shard_map/ppermute | solution.py:25
  40.5 8.4 %collective-permute-done = bf16[4,2,128,512]{3,2,0,1:T(8,128)(2,1)} collective-permute-done((bf16[4,2,128,512]{3,2,0,1:T(8,128)(2,1)S(1)}, bf16[4,2,128,512]{3,2,0,1:T(8,128)(2,1)}, u32[]{:S(2)}, u32[]{:S(2)}) %collective-permute-start) | collective-permute-done | bytes 1048608 | tf_op jit(solution)/shard_map/ppermute | solution.py:22
  52.1 6.9 %gather_fusion = bf16[32,2,128,512]{3,2,1,0:T(8,128)(2,1)} fusion(bf16[12,2,128,512]{3,2,0,1:T(8,128)(2,1)} %pad_maximum_fusion, s32[1024]{0:T(1024)S(1)} %pad_clamp_fusion.1), kind=kCustom, calls=%fused_computation | custom fusion | bytes 16777344 | tf_op jit(solution)/shard_map/gather | solution.py:133
  59.0 14.0 %copy.24 = bf16[4,8,2,128,512]{3,1,4,2,0:T(8,128)(2,1)} copy(bf16[4,8,2,128,512]{4,3,2,1,0:T(8,128)(2,1)} %bitcast.152) | data formatting | bytes 16777216 | tf_op jit(solution)/shard_map/while | solution.py:148
  73.9 47.8 %while.22 = (s32[]{:T(128)}, bf16[4,128,512]{2,1,0:T(8,128)(2,1)}, bf16[4,8,2,128,512]{3,1,4,2,0:T(8,128)(2,1)}, pred[4,8,128]{2,1,0:T(8,128)(4,1)S(1)}, bf16[4,128,512]{1,2,0:T(8,128)(2,1)}, /*index=5*/s32[]{:T(128)}) while((s32[]{:T(128)}, bf16[4,128,512]{2,1,0:T(8,128)(2,1)}, bf16[4,8,2,128,512]{3,1,4,2,0:T(8,128)(2,1)}, ...), condition=%wide.region_5.6_spmd, body=%wide.region_2.5_spmd.sunk | while | flops 274793472 | bytes 28322936 | solution.py:148
  125.5 29.1 %all-gather.5.cloned.1.call-done = bf16[2048,512]{0,1:T(8,128)(2,1)} async-done(((bf16[512,512]{0,1:T(8,128)(2,1)}), bf16[2048,512]{0,1:T(8,128)(2,1)}) %all-gather.5.cloned.1.call-update) | async-done | bytes 2097168 | tf_op jit(solution)/shard_map/all_gather | solution.py:154
  159.4 30.4 %all-gather.3.cloned.1.call-done = bf16[2048,512]{1,0:T(8,128)(2,1)} async-done(((bf16[512,512]{1,0:T(8,128)(2,1)}), bf16[2048,512]{1,0:T(8,128)(2,1)}) %all-gather.3.cloned.1.call-update) | async-done | bytes 2097168 | tf_op jit(solution)/shard_map/all_gather | solution.py:155
  189.9 7.8 %fusion.52 = f32[2048,512]{0,1:T(8,128)} fusion(bf16[512,512]{1,0:T(8,128)(2,1)S(1)} %copy-done, f32[2048,512]{1,0:T(8,128)} %fusion.87, bf16[2048,512]{1,0:T(8,128)(2,1)} %all-gather.3.cloned.1.call-done, bf16[512,512]{1,0:T(8,128)(2,1)S(1)} %copy-done.37), kind=kOutput, calls=%fused_computation.68 | convolution fusion | flops 2167406592 | bytes 11534336 | tf_op jit(solution)/shard_map/dot_general | solution.py:54
  198.9 48.3 %reduce-scatter.2.cloned.1.call-done = f32[512,512]{0,1:T(8,128)} async-done(((f32[2048,512]{0,1:T(8,128)}), f32[512,512]{0,1:T(8,128)}) %reduce-scatter.2.cloned.1.call-update) | async-done | bytes 1048592 | tf_op jit(solution)/shard_map/reduce_scatter | solution.py:160
  251.6 200.1 %while.23 = (s32[]{:T(128)}, bf16[4,128,512]{2,1,0:T(8,128)(2,1)}, f32[4,8,2,128,512]{4,1,0,3,2:T(8,128)}, bf16[4,8,2,128,512]{3,1,4,2,0:T(8,128)(2,1)}, pred[4,...) while((s32[]{:T(128)}, bf16[4,128,512]{2,1,0:T(8,128)(2,1)}, ...), condition=%wide.region_15.16_spmd, body=%wide.region_11.15_spmd.sunk | while | flops 693179392 | bytes 89017480 | solution.py:189
  262.5 11.4 %fusion.162 = bf16[8,64,128]{2,1,0:T(8,128)(2,1)S(1)} fusion(bf16[1024,8,64]{0,2,1:T(8,128)(2,1)S(1)} %copy-done.5, f32[8,128,1024]{2,1,0:T(8,128)} %fusion.160, f32[8,128,1024]{2,1,0:T(8,128)} %get-tuple-element.233, f32[8,128]{1,0:T(8,128)S(1)} %get-tuple-element.234), kind=kOutput, calls=%fused_computation.39.clone.1 | convolution fusion | flops 141625344 | bytes 9572352 | tf_op jit(solution)/shard_map/while/body/eval_jaxpr/hqk,khd->qhd/dot_general | solution.py:179
  274.0 10.8 %fusion.164 = f32[8,64,1024]{2,1,0:T(8,128)S(1)} fusion(bf16[128,8,64]{0,2,1:T(8,128)(2,1)S(1)} %bitcast.156, f32[8,128,1024]{2,1,0:T(8,128)} %fusion.160, f32[8,128,1024]{2,1,0:T(8,128)} %get-tuple-element.233, f32[8,128]{1,0:T(8,128)S(1)} %get-tuple-element.234), kind=kOutput, calls=%fused_computation.28.clone.1 | convolution fusion | flops 141559808 | bytes 10620928 | tf_op jit(solution)/shard_map/while/body/eval_jaxpr/hqk,qhd->khd/dot_general | solution.py:82
  312.6 11.4 %fusion.162 = bf16[8,64,128]{2,1,0:T(8,128)(2,1)S(1)} fusion(bf16[1024,8,64]{0,2,1:T(8,128)(2,1)S(1)} %copy-done.5, f32[8,128,1024]{2,1,0:T(8,128)} %fusion.160, f32[8,128,1024]{2,1,0:T(8,128)} %get-tuple-element.233, f32[8,128]{1,0:T(8,128)S(1)} %get-tuple-element.234), kind=kOutput, calls=%fused_computation.39.clone.1 | convolution fusion | flops 141625344 | bytes 9572352 | tf_op jit(solution)/shard_map/while/body/eval_jaxpr/hqk,khd->qhd/dot_general | solution.py:179
  324.0 10.8 %fusion.164 = f32[8,64,1024]{2,1,0:T(8,128)S(1)} fusion(bf16[128,8,64]{0,2,1:T(8,128)(2,1)S(1)} %bitcast.156, f32[8,128,1024]{2,1,0:T(8,128)} %fusion.160, f32[8,128,1024]{2,1,0:T(8,128)} %get-tuple-element.233, f32[8,128]{1,0:T(8,128)S(1)} %get-tuple-element.234), kind=kOutput, calls=%fused_computation.28.clone.1 | convolution fusion | flops 141559808 | bytes 10620928 | tf_op jit(solution)/shard_map/while/body/eval_jaxpr/hqk,qhd->khd/dot_general | solution.py:82
  362.5 11.4 %fusion.162 = bf16[8,64,128]{2,1,0:T(8,128)(2,1)S(1)} fusion(bf16[1024,8,64]{0,2,1:T(8,128)(2,1)S(1)} %copy-done.5, f32[8,128,1024]{2,1,0:T(8,128)} %fusion.160, f32[8,128,1024]{2,1,0:T(8,128)} %get-tuple-element.233, f32[8,128]{1,0:T(8,128)S(1)} %get-tuple-element.234), kind=kOutput, calls=%fused_computation.39.clone.1 | convolution fusion | flops 141625344 | bytes 9572352 | tf_op jit(solution)/shard_map/while/body/eval_jaxpr/hqk,khd->qhd/dot_general | solution.py:179
  373.9 10.8 %fusion.164 = f32[8,64,1024]{2,1,0:T(8,128)S(1)} fusion(bf16[128,8,64]{0,2,1:T(8,128)(2,1)S(1)} %bitcast.156, f32[8,128,1024]{2,1,0:T(8,128)} %fusion.160, f32[8,128,1024]{2,1,0:T(8,128)} %get-tuple-element.233, f32[8,128]{1,0:T(8,128)S(1)} %get-tuple-element.234), kind=kOutput, calls=%fused_computation.28.clone.1 | convolution fusion | flops 141559808 | bytes 10620928 | tf_op jit(solution)/shard_map/while/body/eval_jaxpr/hqk,qhd->khd/dot_general | solution.py:82
  390.6 5.6 %copy.67 = f32[1,8,2,128,512]{4,1,0,3,2:T(8,128)} copy(f32[1,8,2,128,512]{3,1,4,2,0:T(8,128)} %maximum_bitcast_fusion.2) | data formatting | bytes 8388608 | tf_op jit(solution)/shard_map/while/body/jit(dynamic_update_index_in_dim)/dynamic_update_slice | solution.py:189
  412.5 11.4 %fusion.162 = bf16[8,64,128]{2,1,0:T(8,128)(2,1)S(1)} fusion(bf16[1024,8,64]{0,2,1:T(8,128)(2,1)S(1)} %copy-done.5, f32[8,128,1024]{2,1,0:T(8,128)} %fusion.160, f32[8,128,1024]{2,1,0:T(8,128)} %get-tuple-element.233, f32[8,128]{1,0:T(8,128)S(1)} %get-tuple-element.234), kind=kOutput, calls=%fused_computation.39.clone.1 | convolution fusion | flops 141625344 | bytes 9572352 | tf_op jit(solution)/shard_map/while/body/eval_jaxpr/hqk,khd->qhd/dot_general | solution.py:179
  424.0 10.8 %fusion.164 = f32[8,64,1024]{2,1,0:T(8,128)S(1)} fusion(bf16[128,8,64]{0,2,1:T(8,128)(2,1)S(1)} %bitcast.156, f32[8,128,1024]{2,1,0:T(8,128)} %fusion.160, f32[8,128,1024]{2,1,0:T(8,128)} %get-tuple-element.233, f32[8,128]{1,0:T(8,128)S(1)} %get-tuple-element.234), kind=kOutput, calls=%fused_computation.28.clone.1 | convolution fusion | flops 141559808 | bytes 10620928 | tf_op jit(solution)/shard_map/while/body/eval_jaxpr/hqk,qhd->khd/dot_general | solution.py:82
  440.6 5.6 %copy.67 = f32[1,8,2,128,512]{4,1,0,3,2:T(8,128)} copy(f32[1,8,2,128,512]{3,1,4,2,0:T(8,128)} %maximum_bitcast_fusion.2) | data formatting | bytes 8388608 | tf_op jit(solution)/shard_map/while/body/jit(dynamic_update_index_in_dim)/dynamic_update_slice | solution.py:189
  451.7 9.5 %convolution_bitcast_fusion = f32[12,2,128,512]{3,0,2,1:T(8,128)S(1)} fusion(f32[4,8,2,128,512]{4,1,0,3,2:T(8,128)} %get-tuple-element.72, s32[4,8]{1,0:T(4,128)S(1)} %copy-done.33), kind=kOutput, calls=%fused_computation.63 | convolution fusion | flops 603980160 | bytes 23068800 | tf_op jit(solution)/shard_map/qix,qigzo->xgzo/dot_general | solution.py:194
  464.4 7.9 %collective-permute-start.3 = (f32[4,2,128,512]{3,0,2,1:T(4,128)S(1)}, f32[4,2,128,512]{3,0,2,1:T(4,128)S(1)}, u32[]{:S(2)}, u32[]{:S(2)}) collective-permute-start(f32[4,2,128,512]{3,0,2,1:T(4,128)S(1)} %get-tuple-element.136), channel_id=1, source_target_pairs={{1,0},{2,1},{3,2},{4,3},{5,4},{6,5},{7,6},{8,7},{9,8},{10,9},{11,1... | collective-permute-start | bytes 6291464 | tf_op jit(solution)/shard_map/ppermute | solution.py:25
  472.8 43.0 %collective-permute-done.2 = f32[4,2,128,512]{3,0,2,1:T(4,128)S(1)} collective-permute-done((f32[4,2,128,512]{3,0,2,1:T(4,128)S(1)}, f32[4,2,128,512]{3,0,2,1:T(4,128)S(1)}, u32[]{:S(2)}, u32[]{:S(2)}) %collective-permute-start.2) | collective-permute-done | bytes 2097184 | tf_op jit(solution)/shard_map/ppermute | solution.py:22
  (253 shorter events, 186.8 us)
Async XLA Ops:
  6.5 148.0 %copy-start = (bf16[512,512]{1,0:T(8,128)(2,1)S(1)}, bf16[512,512]{1,0:T(8,128)(2,1)}, u32[]{:S(2)}) copy-start(bf16[512,512]{1,0:T(8,128)(2,1)} %param.25) | copy-start | bytes 1572868
  6.5 148.0 %all-gather.5.cloned.1.call-start = ((), (), s32[]{:S(2)}) async-start(), calls=%async_computation.2 | async-start | bytes 2621440 | tf_op jit(solution)/shard_map/all_gather | solution.py:154
  7.9 113.8 %copy-start.6 = (bf16[512,512]{0,1:T(8,128)(2,1)}, bf16[512,512]{0,1:T(8,128)(2,1)S(1)}, u32[]{:S(2)}) copy-start(bf16[512,512]{0,1:T(8,128)(2,1)S(1)} %copy.23) | copy-start | bytes 1572868
  7.9 12.2 %copy-start.36 = (s32[4,8]{1,0:T(4,128)S(1)}, s32[4,8]{1,0:T(4,128)}, u32[]{:S(2)}) copy-start(s32[4,8]{1,0:T(4,128)} %param.27) | copy-start | bytes 388
  8.0 15.2 %copy-start.25 = (f32[512]{0:T(512)}, f32[512]{0:T(512)S(1)}, u32[]{:S(2)}) copy-start(f32[512]{0:T(512)S(1)} %broadcast_multiply_fusion.5) | copy-start | bytes 6148
  8.2 15.0 %copy-start.27 = (f32[512]{0:T(512)}, f32[512]{0:T(512)S(1)}, u32[]{:S(2)}) copy-start(f32[512]{0:T(512)S(1)} %add_rsqrt_fusion.1) | copy-start | bytes 6148
  9.9 15.4 %copy-start.20 = (s32[512,128]{1,0:T(8,128)S(1)}, s32[512,128]{1,0:T(8,128)}, u32[]{:S(2)}) copy-start(s32[512,128]{1,0:T(8,128)} %param.29) | copy-start | bytes 786436
  9.9 16.0 %copy-start.38 = (s32[4]{0:T(128)S(1)}, s32[4]{0:T(128)}, u32[]{:S(2)}) copy-start(s32[4]{0:T(128)} %param.28) | copy-start | bytes 52
  10.6 30.0 %collective-permute-start.1 = (bf16[4,2,128,512]{3,2,0,1:T(8,128)(2,1)S(1)}, bf16[4,2,128,512]{3,2,0,1:T(8,128)(2,1)}, u32[]{:S(2)}, u32[]{:S(2)}) collective-permute-start(bf16[4,2,128,512]{3,2,0,1:T(8,128)(2,1)S(1)} %pad_maximum_fusion.1), channel_id=1, source_target_pairs={{1,0},{2,1},{3,2},{4,3},{5,4},{6,5},{7,6},{8,7},{9,8},{10,9},{11,1... | collective-permute-start | bytes 3145736 | tf_op jit(solution)/shard_map/ppermute | solution.py:25
  18.1 30.8 %collective-permute-start = (bf16[4,2,128,512]{3,2,0,1:T(8,128)(2,1)S(1)}, bf16[4,2,128,512]{3,2,0,1:T(8,128)(2,1)}, u32[]{:S(2)}, u32[]{:S(2)}) collective-permute-start(bf16[4,2,128,512]{3,2,0,1:T(8,128)(2,1)S(1)} %pad_maximum_fusion.1), channel_id=1, source_target_pairs={{0,1},{1,2},{2,3},{3,4},{4,5},{5,6},{6,7},{7,8},{8,9},{9,10},{10,1... | collective-permute-start | bytes 3145736 | tf_op jit(solution)/shard_map/ppermute | solution.py:22
  73.9 49.8 %copy-start.23 = (f32[512]{0:T(512)S(1)}, f32[512]{0:T(512)}, u32[]{:S(2)}) copy-start(f32[512]{0:T(512)} %param.20) | copy-start | bytes 6148
  123.4 125.3 %copy-start.2 = (f32[512,512]{0,1:T(8,128)}, f32[512,512]{0,1:T(8,128)S(1)}, u32[]{:S(2)}) copy-start(f32[512,512]{0,1:T(8,128)S(1)} %get-tuple-element.141) | copy-start | bytes 3145732
  123.5 125.3 %copy-start.18 = (f32[512]{0:T(512)}, f32[512]{0:T(512)S(1)}, u32[]{:S(2)}) copy-start(f32[512]{0:T(512)S(1)} %broadcast_multiply_fusion.4) | copy-start | bytes 6148
  123.7 125.1 %copy-start.21 = (f32[512]{0:T(512)}, f32[512]{0:T(512)S(1)}, u32[]{:S(2)}) copy-start(f32[512]{0:T(512)S(1)} %add_rsqrt_fusion) | copy-start | bytes 6148
  124.6 65.2 %all-gather.3.cloned.1.call-start = ((), (), s32[]{:S(2)}) async-start(), calls=%async_computation.1 | async-start | bytes 2621440 | tf_op jit(solution)/shard_map/all_gather | solution.py:155
  125.4 64.5 %copy-start.37 = (bf16[512,512]{1,0:T(8,128)(2,1)S(1)}, bf16[512,512]{1,0:T(8,128)(2,1)}, u32[]{:S(2)}) copy-start(bf16[512,512]{1,0:T(8,128)(2,1)} %param.26) | copy-start | bytes 1572868
  125.4 121.8 %reduce-scatter.2.cloned.1.call-start = ((), (), s32[]{:S(2)}) async-start(), calls=%async_computation.3 | async-start | bytes 5242880 | tf_op jit(solution)/shard_map/reduce_scatter | solution.py:160
  197.6 51.1 %copy-start.12 = (bf16[512,512]{1,0:T(8,128)(2,1)S(1)}, bf16[512,512]{1,0:T(8,128)(2,1)}, u32[]{:S(2)}) copy-start(bf16[512,512]{1,0:T(8,128)(2,1)} %param.24) | copy-start | bytes 1572868
  198.9 52.7 %copy-start.9 = (bf16[512,512]{0,1:T(8,128)(2,1)}, bf16[512,512]{0,1:T(8,128)(2,1)S(1)}, u32[]{:S(2)}) copy-start(bf16[512,512]{0,1:T(8,128)(2,1)S(1)} %copy.22) | copy-start | bytes 1572868
  251.6 200.1 %copy-start.33 = (s32[4,8]{1,0:T(4,128)S(1)}, s32[4,8]{1,0:T(4,128)}, u32[]{:S(2)}) copy-start(s32[4,8]{1,0:T(4,128)} %get-tuple-element.126) | copy-start | bytes 388
  461.2 11.1 %copy-start.13 = (bf16[4,128,512]{2,1,0:T(8,128)(2,1)S(1)}, bf16[4,128,512]{2,1,0:T(8,128)(2,1)}, u32[]{:S(2)}) copy-start(bf16[4,128,512]{2,1,0:T(8,128)(2,1)} %get-tuple-element.71) | copy-start | bytes 1572868
  462.2 53.5 %collective-permute-start.2 = (f32[4,2,128,512]{3,0,2,1:T(4,128)S(1)}, f32[4,2,128,512]{3,0,2,1:T(4,128)S(1)}, u32[]{:S(2)}, u32[]{:S(2)}) collective-permute-start(f32[4,2,128,512]{3,0,2,1:T(4,128)S(1)} %get-tuple-element.135), channel_id=1, source_target_pairs={{0,1},{1,2},{2,3},{3,4},{4,5},{5,6},{6,7},{7,8},{8,9},{9,10},{10,1... | collective-permute-start | bytes 6291464 | tf_op jit(solution)/shard_map/ppermute | solution.py:22
  464.4 52.6 %collective-permute-start.3 = (f32[4,2,128,512]{3,0,2,1:T(4,128)S(1)}, f32[4,2,128,512]{3,0,2,1:T(4,128)S(1)}, u32[]{:S(2)}, u32[]{:S(2)}) collective-permute-start(f32[4,2,128,512]{3,0,2,1:T(4,128)S(1)} %get-tuple-element.136), channel_id=1, source_target_pairs={{1,0},{2,1},{3,2},{4,3},{5,4},{6,5},{7,6},{8,7},{9,8},{10,9},{11,1... | collective-permute-start | bytes 6291464 | tf_op jit(solution)/shard_map/ppermute | solution.py:25
  472.8 45.9 %copy-start.17 = (bf16[512,512]{1,0:T(8,128)(2,1)S(1)}, bf16[512,512]{1,0:T(8,128)(2,1)}, u32[]{:S(2)}) copy-start(bf16[512,512]{1,0:T(8,128)(2,1)} %param.22) | copy-start | bytes 1572868
  (28 other events, 71.5 us)
Sparse Core Ops, SparseCore 0:
  124.8 29.7 all-gather.4
  156.4 33.4 all-gather.2
  197.8 49.3 reduce-scatter.1
where the time goes:
time: 535 us; the launch traced here: 529 us
  matrix products  183 us (34%)
  waiting for transfers between devices  176 us (33%)
  local copies, waits for them, and re-layouts  119 us (22%)
  starting transfers between devices  19.6 us (4%)
  other arithmetic  17.4 us (3%)
  between operations  13.7 us (3%)
    ppermute x2, waiting for transfers between devices, with_halo(): lax.ppermute(lax.slice_in_dim(block, block.shape[dim] - width, None, axis...  51.4 us
    reduce_scatter x1, waiting for transfers between devices, body(): lax.psum_scatter(dot_last(grad_act, w_up), 'tensor', scatter_dimension=0,...  48.3 us
    dot_general x4, matrix products, backward(): jnp.einsum('hqk,khd->qhd', grad_score, head_split(near_keys), preferred_e...  45.7 us
    dot_general x4, matrix products, key_value_grads(): jnp.einsum('hqk,qhd->khd', grad_score, head_split(query), preferred_eleme...  43.2 us
    dynamic_update_slice x8, local copies, waits for them, and re-layouts, body(): lax.map(backward, (query_blocks, near_all, live_keys, grad_blocks))  40.8 us
    all_gather x1, waiting for transfers between devices, body(): lax.all_gather(output_gradient, 'tensor', axis=0, tiled=True)  30.4 us
    all_gather x1, waiting for transfers between devices, body(): lax.all_gather(second_normed_rows, 'tensor', axis=0, tiled=True)  29.1 us
    sub x8, matrix products, block_probs(): expo = jnp.exp(scores - top_score)  27.8 us
  transfers between devices with their start and end apart: 7, of which 7 were waited for; matrix products, arithmetic and copies ran while one was open for 2% of the time, Pallas kernels for 0%

commit v1 on v0

v1 whole, which is shorter than its diff:
```python
import functools

import jax
import jax.numpy as jnp
from jax import lax
from jax.experimental import pallas as pl
from jax.experimental.pallas import tpu as pltpu
from jax.sharding import PartitionSpec as P

HEADS = 8
HEAD_DIM = 64
NBR = 8
SPAN = 4
BLK = 128
OWN = 4
EXT = OWN + 2 * SPAN
WIN = 2 * SPAN + 1
GRP = 4
SLAB = GRP * HEAD_DIM
NGRP = HEADS // GRP
STK = GRP * BLK
NIT = OWN * NGRP

NORM_EPS = 1e-05
GELU_C = 0.7978845608028654
GELU_A = 0.044715
FAR = -1e30

f32 = jnp.float32
bf16 = jnp.bfloat16
MESH = pl.DeviceIdType.MESH


def dot(left, right):
    return jnp.dot(left, right, preferred_element_type=f32)


def dot_last(left, right):
    return lax.dot_general(left, right, (((1,), (1,)), ((), ())), preferred_element_type=f32)


def norm_parts(values):
    centre = jnp.mean(values, axis=-1, keepdims=True)
    centred = values - centre
    inverse = lax.rsqrt(jnp.mean(centred * centred, axis=-1, keepdims=True) + NORM_EPS)
    return centred * inverse, inverse


def norm_reverse(upstream, normed, inverse, gain):
    scaled = upstream * gain
    first = jnp.mean(scaled, axis=-1, keepdims=True)
    second = jnp.mean(scaled * normed, axis=-1, keepdims=True)
    return inverse * (scaled - first - normed * second)


def gelu_slope(v):
    square = v * v
    tangent = jnp.tanh(v * (GELU_C + GELU_C * GELU_A * square))
    return 0.5 * (1.0 + tangent) + (0.5 * v) * (1.0 - tangent * tangent) * (
        GELU_C + 3.0 * GELU_C * GELU_A * square
    )


def lanes4(tile):
    return jnp.concatenate([tile] * GRP, axis=1)


def put_stack(dst, index, slab):
    head = lax.broadcasted_iota(jnp.int32, (BLK, SLAB), 1) // HEAD_DIM
    for h in range(GRP):
        dst[index, h * BLK : (h + 1) * BLK, :] = jnp.where(head == h, slab, 0.0).astype(bf16)


def diagonal(wide):
    return jnp.concatenate(
        [
            wide[h * HEAD_DIM : (h + 1) * HEAD_DIM, h * BLK : (h + 1) * BLK]
            for h in range(GRP)
        ],
        axis=0,
    )


def kernel(
    nodes,
    tensors,
    x_ref,
    og_ref,
    ag_ref,
    fg_ref,
    wq_ref,
    wk_ref,
    wv_ref,
    wo_ref,
    wu_hbm,
    wd_hbm,
    nbr_ref,
    cnt_ref,
    nm_ref,
    out_ref,
    halo,
    n1h,
    qm,
    qmr,
    kext,
    vext,
    ktr,
    vtr,
    live,
    vsc,
    vbs,
    vbr,
    wbuf,
    sbuf,
    ebuf,
    att,
    attt,
    stats,
    statr,
    invs,
    mid,
    n2,
    acc,
    gmr,
    dob,
    dor,
    dom,
    domr,
    dsb,
    dq,
    dk,
    dv,
    send,
    recv,
    local,
):
    member = lax.axis_index("member")
    node = lax.axis_index("node")
    tensor = lax.axis_index("tensor")
    total = nodes * tensors
    place = node * tensors + tensor
    after = lax.rem(place + 1, total)
    before = lax.rem(place + total - 1, total)
    right = (member, after // tensors, lax.rem(after, tensors))
    left = (member, before // tensors, lax.rem(before, tensors))
    up = (member, node, lax.rem(tensor + 1, tensors))
    down = (member, node, lax.rem(tensor + tensors - 1, tensors))
    twin = (1 - member, node, tensor)

    barrier = pltpu.get_barrier_semaphore()
    for peer in (right, left, up, down, twin):
        pl.semaphore_signal(barrier, inc=1, device_id=peer, device_id_type=MESH)
    pl.semaphore_wait(barrier, 5)

    def copy(slot, src, dst, peer):
        return pltpu.make_async_remote_copy(
            src_ref=src,
            dst_ref=dst,
            send_sem=send.at[slot],
            recv_sem=recv.at[slot],
            device_id=peer,
            device_id_type=MESH,
        )

    rows_right = copy(0, x_ref, halo.at[0], right)
    rows_left = copy(1, x_ref, halo.at[1], left)
    rows_right.start()
    rows_left.start()
    own_up = pltpu.make_async_copy(wu_hbm, wbuf.at[0, 0], local.at[0])
    own_down = pltpu.make_async_copy(wd_hbm, wbuf.at[0, 1], local.at[1])
    own_up.start()
    own_down.start()

    def valid_row(b, carry):
        def valid_one(c, carry):
            wanted = place * OWN - SPAN + b + c
            hit = jnp.int32(0)
            for j in range(NBR):
                same = (nbr_ref[b, j] == wanted) & (j < cnt_ref[b])
                hit = hit | same.astype(jnp.int32)
            vsc[b * WIN + c] = jnp.where(hit > 0, 0.0, FAR).astype(f32)
            return carry

        return lax.fori_loop(0, WIN, valid_one, carry)

    lax.fori_loop(0, OWN, valid_row, 0)
    for b in range(OWN):
        for e in range(OWN):
            row = b * OWN + e
            low = vsc[b * WIN + e - b] if e >= b else jnp.float32(FAR)
            high = vsc[b * WIN + e - b + 2 * SPAN] if e <= b else jnp.float32(FAR)
            vbs[0, row : row + 1, :] = jnp.full((1, BLK), low, f32)
            vbs[1, row : row + 1, :] = jnp.full((1, BLK), high, f32)
    lists_right = copy(2, vbs.at[1], vbr.at[0], right)
    lists_left = copy(3, vbs.at[0], vbr.at[1], left)
    lists_right.start()
    lists_left.start()

    for e in range(EXT):
        block = jnp.clip(place * OWN - SPAN + e, 0, total * OWN - 1)
        line = jnp.where(nm_ref[pl.ds(block, 1), :] > 0, 0.0, FAR).astype(f32)
        live[e * BLK : (e + 1) * BLK, :] = jnp.broadcast_to(line, (BLK, BLK)).T

    def keys_values(normed, base):
        rows = normed.shape[0]
        base = pl.multiple_of(base, BLK)
        k = dot(normed, wk_ref[...]).astype(bf16)
        v = dot(normed, wv_ref[...]).astype(bf16)
        for g in range(NGRP):
            kg, vg = k[:, g * SLAB : (g + 1) * SLAB], v[:, g * SLAB : (g + 1) * SLAB]
            kext[g, pl.ds(base, rows), :] = kg
            vext[g, pl.ds(base, rows), :] = vg
            ktr[g, :, pl.ds(base, rows)] = kg.T
            vtr[g, :, pl.ds(base, rows)] = vg.T

    def queries(normed, dst, first):
        q = dot(normed, wq_ref[...]).astype(bf16).astype(f32) * HEAD_DIM ** (-0.5)
        for i in range(normed.shape[0] // BLK):
            for g in range(NGRP):
                put_stack(
                    dst,
                    first + i * NGRP + g,
                    q[i * BLK : (i + 1) * BLK, g * SLAB : (g + 1) * SLAB],
                )

    def own_rows(r, carry):
        base = pl.multiple_of(r * 256, 256)
        normed, _ = norm_parts(x_ref[pl.ds(base, 256), :].astype(f32))
        normed = (normed * ag_ref[...]).astype(bf16)
        keys_values(normed, SPAN * BLK + base)
        queries(normed, qm, r * 2 * NGRP)
        return carry

    lax.fori_loop(0, 2, own_rows, 0)

    rows_right.wait_recv()
    rows_left.wait_recv()
    rows_right.wait_send()
    rows_left.wait_send()

    own_up.wait()
    own_down.wait()
    ring_up = copy(4, wbuf.at[0, member], wbuf.at[1, member], up)
    ring_down = copy(5, wbuf.at[0, member], wbuf.at[2, member], down)
    ring_up.start()
    ring_down.start()

    def halo_rows(r, carry):
        side = r // 2
        base = pl.multiple_of(lax.rem(r, 2) * 256, 256)
        normed, _ = norm_parts(halo[side, pl.ds(base, 256), :].astype(f32))
        normed = (normed * ag_ref[...]).astype(bf16)
        n1h[side, pl.ds(base, 256), :] = normed
        keys_values(normed, side * (SPAN + OWN) * BLK + base)
        return carry

    lax.fori_loop(0, 4, halo_rows, 0)

    CH = 3
    CR = CH * BLK

    def window_bias(b, c):
        base = pl.multiple_of(b * BLK, BLK)
        tiles = []
        for j in range(CH):
            tile = live[pl.ds(base + (c * CH + j) * BLK, BLK), :]
            tiles.append(tile + vsc[b * WIN + c * CH + j])
        return lanes4(jnp.concatenate(tiles, axis=0))

    def forward(it, carry):
        b, g = it // NGRP, lax.rem(it, NGRP)
        base = pl.multiple_of(b * BLK, BLK)
        stack = qm[it]
        top = jnp.full((1, STK), 2 * FAR, f32)
        for c in range(WIN // CH):
            s = dot_last(kext[g, pl.ds(base + c * CR, CR), :], stack) + window_bias(b, c)
            sbuf[c * CR : (c + 1) * CR, :] = s
            top = jnp.maximum(top, jnp.max(s, axis=0, keepdims=True))
        count = jnp.zeros((1, STK), f32)
        for c in range(WIN // CH):
            e = jnp.exp(sbuf[c * CR : (c + 1) * CR, :] - top)
            count = count + jnp.sum(e, axis=0, keepdims=True)
            ebuf[it, c * CR : (c + 1) * CR, :] = e.astype(bf16)
        inverse = 1.0 / count
        wide = dot(vtr[g, :, pl.ds(base, WIN * BLK)], ebuf[it]) * inverse
        own = diagonal(wide)
        attt[it] = own
        att[g, pl.ds(base, BLK), :] = own.T.astype(bf16)
        stats[pl.ds(it, 1), :] = top + jnp.log(count)
        invs[pl.ds(it, 1), :] = inverse
        return carry

    lax.fori_loop(0, 6, forward, 0)

    ring_up.wait_recv()
    ring_down.wait_recv()
    cross_up = copy(
        6, wbuf.at[1, member, pl.ds(0, 256)], wbuf.at[3, member, pl.ds(0, 256)], up
    )
    cross_down = copy(
        7, wbuf.at[2, member, pl.ds(256, 256)], wbuf.at[3, member, pl.ds(256, 256)], down
    )
    cross_up.start()
    cross_down.start()
    twin_one = copy(8, wbuf.at[1, member], wbuf.at[1, member], twin)
    twin_two = copy(9, wbuf.at[2, member], wbuf.at[2, member], twin)
    twin_one.start()
    twin_two.start()

    lax.fori_loop(6, NIT, forward, 0)

    def middle(r, carry):
        rows = pl.ds(pl.multiple_of(r * 256, 256), 256)
        value = x_ref[rows, :].astype(f32) + (
            dot(att[0, rows, :], wo_ref[0:SLAB, :]) + dot(att[1, rows, :], wo_ref[SLAB:, :])
        )
        mid[rows, :] = value
        normed, _ = norm_parts(value)
        n2[rows, :] = (normed * fg_ref[...]).astype(bf16)
        acc[rows, :] = jnp.zeros((256, acc.shape[1]), f32)
        return carry

    lax.fori_loop(0, 2, middle, 0)

    def hidden(slot):
        def run(r, carry):
            rows = pl.ds(pl.multiple_of(r * 256, 256), 256)
            pre = dot(n2[rows, :], wbuf[slot, 0])
            slope = gelu_slope(pre)
            grad = dot_last(og_ref[rows, :], wbuf[slot, 1])
            act = (grad * slope).astype(bf16)
            acc[rows, :] += dot_last(act, wbuf[slot, 0])
            return carry

        lax.fori_loop(0, 2, run, 0)

    other = 1 - member

    def arrival(slot_id, slot, part):
        return copy(slot_id, wbuf.at[slot, other, part], wbuf.at[slot, other, part], twin)

    hidden(0)
    arrival(8, 1, pl.ds(0, 512)).wait_recv()
    hidden(1)
    cross_up.wait_recv()
    cross_down.wait_recv()
    twin_three = copy(10, wbuf.at[3, member], wbuf.at[3, member], twin)
    twin_three.start()
    arrival(9, 2, pl.ds(0, 512)).wait_recv()
    hidden(2)
    arrival(10, 3, pl.ds(0, 512)).wait_recv()
    hidden(3)

    for b in range(OWN):
        rows = slice(b * BLK, (b + 1) * BLK)
        up_grad = og_ref[rows, :].astype(f32)
        normed, inverse = norm_parts(mid[rows, :])
        res = up_grad + norm_reverse(acc[rows, :], normed, inverse, fg_ref[...])
        gmr[rows, :] = res
        res_bf = res.astype(bf16)
        n2[rows, :] = res_bf
        grad_att = dot_last(res_bf, wo_ref[...]).astype(bf16)
        dob[rows, :] = grad_att
        grad_wide = grad_att.astype(f32)
        grad_t = dot_last(wo_ref[...], res_bf).astype(bf16).astype(f32)
        for g in range(NGRP):
            it = b * NGRP + g
            put_stack(dom, it, grad_wide[:, g * SLAB : (g + 1) * SLAB])
            product = grad_t[g * SLAB : (g + 1) * SLAB, :] * attt[it]
            stats[NIT + it : NIT + it + 1, :] = jnp.concatenate(
                [
                    jnp.sum(product[h * HEAD_DIM : (h + 1) * HEAD_DIM], axis=0, keepdims=True)
                    for h in range(GRP)
                ],
                axis=1,
            )

    grads_right = copy(11, dob, dor.at[0], right)
    grads_left = copy(12, dob, dor.at[1], left)
    stats_right = copy(13, stats, statr.at[0], right)
    stats_left = copy(14, stats, statr.at[1], left)
    stats_right.start()
    stats_left.start()
    grads_right.start()
    grads_left.start()

    dk[...] = jnp.zeros(dk.shape, f32)
    dv[...] = jnp.zeros(dv.shape, f32)

    def backward(it, carry):
        b, g = it // NGRP, lax.rem(it, NGRP)
        base = pl.multiple_of(b * BLK, BLK)
        grad_stack = dom[it]
        inverse = invs[pl.ds(it, 1), :]
        centre = stats[pl.ds(NIT + it, 1), :]
        for c in range(WIN // CH):
            rows = slice(c * CR, (c + 1) * CR)
            grad_prob = dot_last(vext[g, pl.ds(base + c * CR, CR), :], grad_stack)
            probs = ebuf[it, rows, :].astype(f32) * inverse
            ebuf[it, rows, :] = probs.astype(bf16)
            dsb[rows, :] = (probs * (grad_prob - centre)).astype(bf16)
        wide = dot(ktr[g, :, pl.ds(base, WIN * BLK)], dsb[...])
        dq[g, pl.ds(base, BLK), :] = (diagonal(wide) * HEAD_DIM ** (-0.5)).T.astype(bf16)
        own = pl.ds(pl.multiple_of((SPAN - b) * BLK, BLK), OWN * BLK)
        dk[g] += dot(dsb[own, :], qm[it])
        dv[g] += dot(ebuf[it, own, :], grad_stack)
        return carry

    lax.fori_loop(0, NIT, backward, 0)

    def far_queries(r, carry):
        side = r // 2
        base = pl.multiple_of(lax.rem(r, 2) * 256, 256)
        queries(n1h[side, pl.ds(base, 256), :], qmr, r * 2 * NGRP)
        return carry

    lax.fori_loop(0, 4, far_queries, 0)

    lists_right.wait_recv()
    lists_left.wait_recv()
    stats_right.wait_recv()
    stats_left.wait_recv()
    grads_right.wait_recv()
    grads_left.wait_recv()

    for side in range(2):
        for b in range(OWN):
            for g in range(NGRP):
                put_stack(
                    domr,
                    (side * OWN + b) * NGRP + g,
                    dor[side, b * BLK : (b + 1) * BLK, g * SLAB : (g + 1) * SLAB].astype(f32),
                )

    for side in range(2):
        for b in range(OWN):
            first, last = (0, b + 1) if side == 0 else (b, OWN)

            def remote(g, carry, side=side, b=b, first=first, last=last):
                it = b * NGRP + g
                stack = qmr[side * NIT + it]
                grad_stack = domr[side * NIT + it]
                level = statr[side, pl.ds(it, 1), :]
                centre = statr[side, pl.ds(NIT + it, 1), :]
                rows = slice(first * BLK, last * BLK)
                ext = slice((SPAN + first) * BLK, (SPAN + last) * BLK)
                s = dot_last(kext[g, ext, :], stack)
                shift = []
                for c in range(first, last):
                    row = b * OWN + c
                    listed = lanes4(vbr[side, row : row + 1, :]) - level
                    part = s[(c - first) * BLK : (c - first + 1) * BLK, :]
                    shift.append(
                        part + (lanes4(live[(SPAN + c) * BLK : (SPAN + c + 1) * BLK, :]) + listed)
                    )
                probs = jnp.exp(jnp.concatenate(shift, axis=0))
                grad_prob = dot_last(vext[g, ext, :], grad_stack)
                grad_score = (probs * (grad_prob - centre)).astype(bf16)
                dk[g, rows, :] += dot(grad_score, stack)
                dv[g, rows, :] += dot(probs.astype(bf16), grad_stack)
                return carry

            lax.fori_loop(0, NGRP, remote, 0)

    def finish(r, carry):
        rows = pl.ds(pl.multiple_of(r * 256, 256), 256)
        grad = None
        for g in range(NGRP):
            cols = slice(g * SLAB, (g + 1) * SLAB)
            term = dot_last(dq[g, rows, :], wq_ref[:, cols])
            term += dot_last(dk[g, rows, :].astype(bf16), wk_ref[:, cols])
            term += dot_last(dv[g, rows, :].astype(bf16), wv_ref[:, cols])
            grad = term if grad is None else grad + term
        normed, inverse = norm_parts(x_ref[rows, :].astype(f32))
        out_ref[rows, :] = (
            gmr[rows, :] + norm_reverse(grad, normed, inverse, ag_ref[...])
        ).astype(out_ref.dtype)
        return carry

    lax.fori_loop(0, 2, finish, 0)

    for done in (
        lists_right,
        lists_left,
        ring_up,
        ring_down,
        cross_up,
        cross_down,
        twin_one,
        twin_two,
        twin_three,
        stats_right,
        stats_left,
        grads_right,
        grads_left,
    ):
        done.wait_send()


def body(nodes, tensors, *args):
    (x, og, ag, fg, wq, wk, wv, wo, wu, wd, nbr, cnt, nm) = args
    rows, width = x.shape
    vm = pl.BlockSpec(memory_space=pltpu.VMEM)
    sm = pl.BlockSpec(memory_space=pltpu.SMEM)
    hbm = pl.BlockSpec(memory_space=pl.ANY)
    V = pltpu.VMEM
    return pl.pallas_call(
        functools.partial(kernel, nodes, tensors),
        out_shape=jax.ShapeDtypeStruct((rows, width), bf16),
        in_specs=[vm] * 8 + [hbm] * 2 + [sm] * 2 + [vm],
        out_specs=vm,
        scratch_shapes=[
            V((2, rows, width), bf16),
            V((2, rows, width), bf16),
            V((NIT, STK, SLAB), bf16),
            V((2 * NIT, STK, SLAB), bf16),
            V((NGRP, EXT * BLK, SLAB), bf16),
            V((NGRP, EXT * BLK, SLAB), bf16),
            V((NGRP, SLAB, EXT * BLK), bf16),
            V((NGRP, SLAB, EXT * BLK), bf16),
            V((EXT * BLK, BLK), f32),
            pltpu.SMEM((OWN * WIN,), f32),
            V((2, OWN * OWN, BLK), f32),
            V((2, OWN * OWN, BLK), f32),
            V((4, 2, width, width), bf16),
            V((WIN * BLK, STK), f32),
            V((NIT, WIN * BLK, STK), bf16),
            V((NGRP, rows, SLAB), bf16),
            V((NIT, SLAB, BLK), f32),
            V((2 * NIT, STK), f32),
            V((2, 2 * NIT, STK), f32),
            V((NIT, STK), f32),
            V((rows, width), f32),
            V((rows, width), bf16),
            V((rows, width), f32),
            V((rows, width), f32),
            V((rows, width), bf16),
            V((2, rows, width), bf16),
            V((NIT, STK, SLAB), bf16),
            V((2 * NIT, STK, SLAB), bf16),
            V((WIN * BLK, STK), bf16),
            V((NGRP, rows, SLAB), bf16),
            V((NGRP, rows, SLAB), f32),
            V((NGRP, rows, SLAB), f32),
            pltpu.SemaphoreType.DMA((15,)),
            pltpu.SemaphoreType.DMA((15,)),
            pltpu.SemaphoreType.DMA((2,)),
        ],
        compiler_params=pltpu.CompilerParams(
            collective_id=0, has_side_effects=True, vmem_limit_bytes=60 * 1024 * 1024
        ),
    )(x, og, ag.reshape(1, width), fg.reshape(1, width), wq, wk, wv, wo, wu, wd, nbr, cnt, nm)


def solution(mesh):
    return jax.shard_map(
        functools.partial(body, mesh.shape["node"], mesh.shape["tensor"]),
        mesh=mesh,
        in_specs=(
            P(("member", "node", "tensor"), None),
            P(("member", "node", "tensor"), None),
            P(),
            P(),
            P(),
            P(),
            P(),
            P(),
            P(None, "tensor"),
            P("tensor", None),
            P(("node", "tensor"), None),
            P(("node", "tensor")),
            P(),
        ),
        out_specs=P(("member", "node", "tensor"), None),
        check_vma=False,
    )
```

time: 535 us -> 84.4 us (0.16)
  the two profiles are of different devices: /device:TPU:160 before, /device:TPU:1 now
where the time goes in v1:
time: 84.4 us; the launch traced here: 84.3 us
  Pallas kernels  82.4 us (98%)
  local copies, waits for them, and re-layouts  1.87 us (2%)
    pallas_call x1, Pallas kernels, body(): pl.pallas_call(functools.partial(kernel, nodes, tensors), out_shape=jax.S...  82.4 us
    unnamed x1, local copies, waits for them, and re-layouts  1.87 us

profile of v1, /device:TPU:1, one launch (start us, length us, event | category | flops | bytes accessed | tf_op | source)
XLA Modules:
  0.0 84.3 jit_solution(2137163195740158700)
XLA Ops:
  0.0 82.4 %shard_map.127 = bf16[512,512]{1,0:T(8,128)(2,1)} custom-call(bf16[512,512]{1,0:T(8,128)(2,1)} %x_ref.1, bf16[512,512]{1,0:T(8,128)(2,1)} %og_ref.1, f32[1,512]{1,0:T(1,128)} %bitcast.2, f32[1,512]{1,0:T(1,128)} %bitcast.3, bf16[512,512]{1,0:T(8,128)(2,1)} %wq_ref.1, bf16[512,512]{1,0:T(8,128)(2,1)} %wk_ref.1, bf16[512,512]{1,0:T(8,128)(2,1)} %wv_ref.1, ...), custom_call_target="tpu_custom_call" | custom-call | tf_op jit(solution)/shard_map/pallas_call | solution.py:507
  82.4 1.9 %copy.15 = bf16[512,512]{1,0:T(8,128)(2,1)} copy(bf16[512,512]{1,0:T(8,128)(2,1)} %shard_map.127) | data formatting | bytes 1048576

commit v2 on v1

v2 whole, which is shorter than its diff:
```python
import functools

import jax
import jax.numpy as jnp
from jax import lax
from jax.experimental import pallas as pl
from jax.experimental.pallas import tpu as pltpu
from jax.sharding import PartitionSpec as P

HEADS = 8
HEAD_DIM = 64
NBR = 8
SPAN = 4
BLK = 128
OWN = 4
HWIN = SPAN + 1
GRP = 4
SLAB = GRP * HEAD_DIM
NGRP = HEADS // GRP
STK = GRP * BLK
NIT = OWN * NGRP

NORM_EPS = 1e-05
GELU_C = 0.7978845608028654
GELU_A = 0.044715
FAR = -1e30

f32 = jnp.float32
bf16 = jnp.bfloat16
MESH = pl.DeviceIdType.MESH


def dot(left, right):
    return jnp.dot(left, right, preferred_element_type=f32)


def dot_last(left, right):
    return lax.dot_general(left, right, (((1,), (1,)), ((), ())), preferred_element_type=f32)


def norm_parts(values):
    centre = jnp.mean(values, axis=-1, keepdims=True)
    centred = values - centre
    inverse = lax.rsqrt(jnp.mean(centred * centred, axis=-1, keepdims=True) + NORM_EPS)
    return centred * inverse, inverse


def norm_reverse(upstream, normed, inverse, gain):
    scaled = upstream * gain
    first = jnp.mean(scaled, axis=-1, keepdims=True)
    second = jnp.mean(scaled * normed, axis=-1, keepdims=True)
    return inverse * (scaled - first - normed * second)


def gelu_slope(v):
    square = v * v
    tangent = jnp.tanh(v * (GELU_C + GELU_C * GELU_A * square))
    return 0.5 * (1.0 + tangent) + (0.5 * v) * (1.0 - tangent * tangent) * (
        GELU_C + 3.0 * GELU_C * GELU_A * square
    )


def lanes4(tile):
    return jnp.concatenate([tile] * GRP, axis=1)


def put_stack(dst, index, slab):
    head = lax.broadcasted_iota(jnp.int32, (BLK, SLAB), 1) // HEAD_DIM
    for h in range(GRP):
        dst[index, h * BLK : (h + 1) * BLK, :] = jnp.where(head == h, slab, 0.0).astype(bf16)


def diagonal(wide):
    return jnp.concatenate(
        [
            wide[h * HEAD_DIM : (h + 1) * HEAD_DIM, h * BLK : (h + 1) * BLK]
            for h in range(GRP)
        ],
        axis=0,
    )


def kernel(
    nodes,
    tensors,
    x_hbm,
    og_hbm,
    ag_ref,
    fg_ref,
    wq_hbm,
    wk_hbm,
    wv_hbm,
    wo_hbm,
    wu_hbm,
    wd_hbm,
    nbr_ref,
    cnt_ref,
    nm_hbm,
    out_ref,
    x_ref,
    og_ref,
    wq_ref,
    wk_ref,
    wv_ref,
    wo_ref,
    nm_ref,
    halo,
    n1h,
    qm,
    qmr,
    kown,
    vown,
    ktown,
    vtown,
    khal,
    vhal,
    kthal,
    vthal,
    live,
    vsc,
    vbs,
    vbr,
    wbuf,
    sbuf,
    eown,
    ehal,
    att,
    attt,
    top_one,
    count_one,
    lse,
    lser,
    centre,
    centrer,
    inv_own,
    inv_hal,
    mid,
    n2,
    acc,
    gmr,
    dob,
    dor,
    dom,
    domr,
    prem,
    dq,
    dk,
    dv,
    send,
    recv,
    local,
):
    member = lax.axis_index("member")
    node = lax.axis_index("node")
    tensor = lax.axis_index("tensor")
    total = nodes * tensors
    place = node * tensors + tensor
    has_left = place > 0
    has_right = place < total - 1
    after = lax.rem(place + 1, total)
    before = lax.rem(place + total - 1, total)
    right = (member, after // tensors, lax.rem(after, tensors))
    left = (member, before // tensors, lax.rem(before, tensors))
    up = (member, node, lax.rem(tensor + 1, tensors))
    down = (member, node, lax.rem(tensor + tensors - 1, tensors))
    twin = (1 - member, node, tensor)

    loads = {}
    for i, (name, src, dst) in enumerate(
        (
            ("x", x_hbm, x_ref),
            ("wk", wk_hbm, wk_ref),
            ("wv", wv_hbm, wv_ref),
            ("wq", wq_hbm, wq_ref),
            ("nm", nm_hbm, nm_ref),
            ("wu", wu_hbm, wbuf.at[0, 0]),
            ("wd", wd_hbm, wbuf.at[0, 1]),
            ("wo", wo_hbm, wo_ref),
            ("og", og_hbm, og_ref),
        )
    ):
        loads[name] = pltpu.make_async_copy(src, dst, local.at[i])
        loads[name].start()

    barrier = pltpu.get_barrier_semaphore()
    for peer in (up, down, twin):
        pl.semaphore_signal(barrier, inc=1, device_id=peer, device_id_type=MESH)

    @pl.when(has_right)
    def _():
        pl.semaphore_signal(barrier, inc=1, device_id=right, device_id_type=MESH)

    @pl.when(has_left)
    def _():
        pl.semaphore_signal(barrier, inc=1, device_id=left, device_id_type=MESH)

    pl.semaphore_wait(barrier, 3 + has_right.astype(jnp.int32) + has_left.astype(jnp.int32))

    def copy(slot, src, dst, peer):
        return pltpu.make_async_remote_copy(
            src_ref=src,
            dst_ref=dst,
            send_sem=send.at[slot],
            recv_sem=recv.at[slot],
            device_id=peer,
            device_id_type=MESH,
        )

    class Pair:
        def __init__(self, slot, to_right, to_left, dst):
            self.to_right = lambda: copy(slot, to_right, dst.at[0], right)
            self.to_left = lambda: copy(slot + 1, to_left, dst.at[1], left)

        def each(self, right_one, left_one, do):
            @pl.when(right_one)
            def _():
                do(self.to_right())

            @pl.when(left_one)
            def _():
                do(self.to_left())

        def start(self):
            self.each(has_right, has_left, lambda c: c.start())

        def wait_send(self):
            self.each(has_right, has_left, lambda c: c.wait_send())

        def wait_recv(self):
            self.each(has_left, has_right, lambda c: c.wait_recv())

    rows = Pair(0, x_hbm, x_hbm, halo)
    rows.start()

    def listed(b, wanted):
        hit = jnp.int32(0)
        for j in range(NBR):
            same = (nbr_ref[b, j] == wanted) & (j < cnt_ref[b])
            hit = hit | same.astype(jnp.int32)
        return jnp.where(hit > 0, 0.0, FAR).astype(f32)

    def valid_row(b, carry):
        for c in range(OWN):
            vsc[b * OWN + c] = listed(b, place * OWN + c)
        for j in range(HWIN):
            e = b + j
            vsc[OWN * OWN + b * HWIN + j] = listed(
                b, place * OWN + jnp.where(e < SPAN, e - SPAN, e - SPAN + OWN)
            )
        return carry

    lax.fori_loop(0, OWN, valid_row, 0)
    for b in range(OWN):
        for e in range(OWN):
            row = b * OWN + e
            base = OWN * OWN + b * HWIN
            low = vsc[base + e - b] if e >= b else jnp.float32(FAR)
            high = vsc[base + SPAN + e - b] if e <= b else jnp.float32(FAR)
            vbs[0, row : row + 1, :] = jnp.full((1, BLK), low, f32)
            vbs[1, row : row + 1, :] = jnp.full((1, BLK), high, f32)
    lists = Pair(2, vbs.at[1], vbs.at[0], vbr)
    lists.start()

    @pl.when(jnp.logical_not(has_left))
    def _():
        vbr[0] = jnp.full(vbr.shape[1:], FAR, f32)
        lser[0] = jnp.zeros(lser.shape[1:], f32)
        centrer[0] = jnp.zeros(centrer.shape[1:], f32)
        halo[0] = jnp.zeros(halo.shape[1:], bf16)
        dor[0] = jnp.zeros(dor.shape[1:], bf16)

    @pl.when(jnp.logical_not(has_right))
    def _():
        vbr[1] = jnp.full(vbr.shape[1:], FAR, f32)
        lser[1] = jnp.zeros(lser.shape[1:], f32)
        centrer[1] = jnp.zeros(centrer.shape[1:], f32)
        halo[1] = jnp.zeros(halo.shape[1:], bf16)
        dor[1] = jnp.zeros(dor.shape[1:], bf16)

    def keys_values(normed, base, k_dst, v_dst, kt_dst, vt_dst):
        count = normed.shape[0]
        base = pl.multiple_of(base, BLK)
        k = dot(normed, wk_ref[...]).astype(bf16)
        v = dot(normed, wv_ref[...]).astype(bf16)
        for g in range(NGRP):
            kg, vg = k[:, g * SLAB : (g + 1) * SLAB], v[:, g * SLAB : (g + 1) * SLAB]
            k_dst[g, pl.ds(base, count), :] = kg
            v_dst[g, pl.ds(base, count), :] = vg
            kt_dst[g, :, pl.ds(base, count)] = kg.T
            vt_dst[g, :, pl.ds(base, count)] = vg.T

    def queries(normed, dst, first):
        q = dot(normed, wq_ref[...]).astype(bf16).astype(f32) * HEAD_DIM ** (-0.5)
        for i in range(normed.shape[0] // BLK):
            for g in range(NGRP):
                put_stack(
                    dst,
                    first + i * NGRP + g,
                    q[i * BLK : (i + 1) * BLK, g * SLAB : (g + 1) * SLAB],
                )

    for name in ("x", "wk", "wv", "wq"):
        loads[name].wait()

    def own_rows(r, carry):
        base = pl.multiple_of(r * 256, 256)
        normed, _ = norm_parts(x_ref[pl.ds(base, 256), :].astype(f32))
        normed = (normed * ag_ref[...]).astype(bf16)
        keys_values(normed, base, kown, vown, ktown, vtown)
        queries(normed, qm, r * 2 * NGRP)
        return carry

    lax.fori_loop(0, 2, own_rows, 0, unroll=True)

    loads["nm"].wait()
    for i in range(OWN + 2 * SPAN):
        e = i if i < OWN else (i - OWN - SPAN if i < OWN + SPAN else i - SPAN)
        block = jnp.clip(place * OWN + e, 0, total * OWN - 1)
        line = jnp.where(nm_ref[pl.ds(block, 1), :] > 0, 0.0, FAR).astype(f32)
        live[i * BLK : (i + 1) * BLK, :] = jnp.broadcast_to(line, (BLK, BLK)).T

    def scores(b, g, blocks, keys, first, flags):
        s = dot_last(keys, qm[b * NGRP + g])
        top = jnp.full((1, STK), 4 * FAR, f32)
        for c in range(blocks):
            bias = live[pl.ds(first + c * BLK, BLK), :] + vsc[flags + c]
            part = s[c * BLK : (c + 1) * BLK, :] + lanes4(bias)
            sbuf[g, c * BLK : (c + 1) * BLK, :] = part
            top = jnp.maximum(top, jnp.max(part, axis=0, keepdims=True))
        return top

    def exponentials(b, g, blocks, top, dst):
        count = jnp.zeros((1, STK), f32)
        for c in range(blocks):
            e = jnp.exp(sbuf[g, c * BLK : (c + 1) * BLK, :] - top)
            count = count + jnp.sum(e, axis=0, keepdims=True)
            dst[b * NGRP + g, c * BLK : (c + 1) * BLK, :] = e.astype(bf16)
        return count

    def per_head(slab, row):
        return jnp.concatenate(
            [
                slab[h * HEAD_DIM : (h + 1) * HEAD_DIM, :] * row[:, h * BLK : (h + 1) * BLK]
                for h in range(GRP)
            ],
            axis=0,
        )

    def forward_own(b, carry):
        tops = [scores(b, g, OWN, kown[g], 0, b * OWN) for g in range(NGRP)]
        counts = [exponentials(b, g, OWN, tops[g], eown) for g in range(NGRP)]
        for g in range(NGRP):
            it = b * NGRP + g
            attt[it] = diagonal(dot(vtown[g], eown[it]))
            top_one[pl.ds(it, 1), :] = tops[g]
            count_one[pl.ds(it, 1), :] = counts[g]
        return carry

    lax.fori_loop(0, OWN, forward_own, 0, unroll=True)

    loads["wu"].wait()
    loads["wd"].wait()
    rows.wait_send()
    ring_up = copy(4, wbuf.at[0, member], wbuf.at[1, member], up)
    ring_down = copy(5, wbuf.at[0, member], wbuf.at[2, member], down)
    ring_up.start()
    ring_down.start()
    rows.wait_recv()

    def halo_rows(r, carry):
        side = r // 2
        base = pl.multiple_of(lax.rem(r, 2) * 256, 256)
        normed, _ = norm_parts(halo[side, pl.ds(base, 256), :].astype(f32))
        normed = (normed * ag_ref[...]).astype(bf16)
        n1h[side, pl.ds(base, 256), :] = normed
        keys_values(normed, side * SPAN * BLK + base, khal, vhal, kthal, vthal)
        return carry

    lax.fori_loop(0, 4, halo_rows, 0, unroll=True)

    def window(ref, b, g):
        return ref[g, pl.ds(pl.multiple_of(b * BLK, BLK), HWIN * BLK), :]

    def window_t(ref, b, g):
        return ref[g, :, pl.ds(pl.multiple_of(b * BLK, BLK), HWIN * BLK)]

    def forward_halo(b, carry):
        first = pl.multiple_of(b * BLK, BLK) + OWN * BLK
        tops = [
            scores(b, g, HWIN, window(khal, b, g), first, OWN * OWN + b * HWIN)
            for g in range(NGRP)
        ]
        counts = [exponentials(b, g, HWIN, tops[g], ehal) for g in range(NGRP)]
        for g in range(NGRP):
            it = b * NGRP + g
            far = diagonal(dot(window_t(vthal, b, g), ehal[it]))
            near_top = top_one[pl.ds(it, 1), :]
            top = jnp.maximum(near_top, tops[g])
            near = jnp.exp(near_top - top)
            distant = jnp.exp(tops[g] - top)
            count = count_one[pl.ds(it, 1), :] * near + counts[g] * distant
            inverse = 1.0 / count
            near = near * inverse
            distant = distant * inverse
            mixed = per_head(attt[it], near) + per_head(far, distant)
            attt[it] = mixed
            att[g, pl.ds(pl.multiple_of(b * BLK, BLK), BLK), :] = mixed.T.astype(bf16)
            lse[pl.ds(it, 1), :] = top + jnp.log(count)
            inv_own[pl.ds(it, 1), :] = near
            inv_hal[pl.ds(it, 1), :] = distant
        return carry

    lax.fori_loop(0, OWN, forward_halo, 0, unroll=True)

    levels = Pair(11, lse, lse, lser)
    levels.start()

    loads["wo"].wait()

    def middle(r, carry):
        part = pl.ds(pl.multiple_of(r * 256, 256), 256)
        value = x_ref[part, :].astype(f32) + (
            dot(att[0, part, :], wo_ref[0:SLAB, :]) + dot(att[1, part, :], wo_ref[SLAB:, :])
        )
        mid[part, :] = value
        normed, _ = norm_parts(value)
        n2[part, :] = (normed * fg_ref[...]).astype(bf16)
        acc[part, :] = jnp.zeros((256, acc.shape[1]), f32)
        return carry

    lax.fori_loop(0, 2, middle, 0, unroll=True)
    loads["og"].wait()

    def hidden(slot):
        def run(r, carry):
            part = pl.ds(pl.multiple_of(r * 256, 256), 256)
            pre = dot(n2[part, :], wbuf[slot, 0])
            slope = gelu_slope(pre)
            grad = dot_last(og_ref[part, :], wbuf[slot, 1])
            act = (grad * slope).astype(bf16)
            acc[part, :] += dot_last(act, wbuf[slot, 0])
            return carry

        lax.fori_loop(0, 2, run, 0, unroll=True)

    other = 1 - member

    def arrival(slot_id, slot):
        return copy(slot_id, wbuf.at[slot, other], wbuf.at[slot, other], twin)

    ring_up.wait_recv()
    ring_down.wait_recv()
    cross_up = copy(
        6, wbuf.at[1, member, pl.ds(0, 256)], wbuf.at[3, member, pl.ds(0, 256)], up
    )
    cross_down = copy(
        7, wbuf.at[2, member, pl.ds(256, 256)], wbuf.at[3, member, pl.ds(256, 256)], down
    )
    cross_up.start()
    cross_down.start()
    twin_one = copy(8, wbuf.at[1, member], wbuf.at[1, member], twin)
    twin_two = copy(9, wbuf.at[2, member], wbuf.at[2, member], twin)
    twin_one.start()
    twin_two.start()

    hidden(0)

    def far_queries(r, carry):
        side = r // 2
        base = pl.multiple_of(lax.rem(r, 2) * 256, 256)
        queries(n1h[side, pl.ds(base, 256), :], qmr, r * 2 * NGRP)
        return carry

    lax.fori_loop(0, 4, far_queries, 0, unroll=True)
    arrival(8, 1).wait_recv()
    hidden(1)
    arrival(9, 2).wait_recv()
    hidden(2)

    pairs = []
    for side in range(2):
        begin = 0
        for b in range(OWN):
            first, last = (0, b + 1) if side == 0 else (b, OWN)
            pairs.append((side, b, first, last, begin * BLK))
            begin += last - first

    lists.wait_recv()
    levels.wait_recv()
    for side, b, first, last, begin in pairs:

        def remote_probs(g, carry, side=side, b=b, first=first, last=last, begin=begin):
            it = b * NGRP + g
            level = lser[side, pl.ds(it, 1), :]
            s = dot_last(kown[g, first * BLK : last * BLK, :], qmr[side * NIT + it])
            for c in range(first, last):
                at = (c - first) * BLK
                row = b * OWN + c
                shift = lanes4(vbr[side, row : row + 1, :]) - level
                bias = lanes4(live[c * BLK : (c + 1) * BLK, :]) + shift
                prem[side, g, begin + at : begin + at + BLK, :] = jnp.exp(
                    s[at : at + BLK, :] + bias
                ).astype(bf16)
            return carry

        lax.fori_loop(0, NGRP, remote_probs, 0, unroll=True)

    cross_up.wait_recv()
    cross_down.wait_recv()
    twin_three = copy(10, wbuf.at[3, member], wbuf.at[3, member], twin)
    twin_three.start()
    arrival(10, 3).wait_recv()
    hidden(3)

    for r in range(2):
        part = slice(r * 256, (r + 1) * 256)
        up_grad = og_ref[part, :].astype(f32)
        normed, inverse = norm_parts(mid[part, :])
        res = up_grad + norm_reverse(acc[part, :], normed, inverse, fg_ref[...])
        gmr[part, :] = res
        res_bf = res.astype(bf16)
        n2[part, :] = res_bf
        dob[part, :] = dot_last(res_bf, wo_ref[...]).astype(bf16)

    grads = Pair(13, dob, dob, dor)
    grads.start()

    for r in range(2):
        part = slice(r * 256, (r + 1) * 256)
        grad_wide = dob[part, :].astype(f32)
        grad_t = dot_last(wo_ref[...], n2[part, :]).astype(bf16).astype(f32)
        for i in range(2):
            for g in range(NGRP):
                it = (r * 2 + i) * NGRP + g
                cols = slice(g * SLAB, (g + 1) * SLAB)
                here = slice(i * BLK, (i + 1) * BLK)
                put_stack(dom, it, grad_wide[here, cols])
                product = grad_t[cols, here] * attt[it]
                centre[it : it + 1, :] = jnp.concatenate(
                    [
                        jnp.sum(
                            product[h * HEAD_DIM : (h + 1) * HEAD_DIM], axis=0, keepdims=True
                        )
                        for h in range(GRP)
                    ],
                    axis=1,
                )

    middles = Pair(15, centre, centre, centrer)
    middles.start()

    dk[...] = jnp.zeros(dk.shape, f32)
    dv[...] = jnp.zeros(dv.shape, f32)

    def backward(b, carry):
        for g in range(NGRP):
            it = b * NGRP + g
            grad_stack = dom[it]
            middle_row = centre[pl.ds(it, 1), :]
            grad_prob = dot_last(vown[g], grad_stack)
            probs = eown[it].astype(f32) * inv_own[pl.ds(it, 1), :]
            grad_score = (probs * (grad_prob - middle_row)).astype(bf16)
            dk[g] += dot(grad_score, qm[it])
            dv[g] += dot(probs.astype(bf16), grad_stack)
            wide = dot(ktown[g], grad_score)
            grad_prob = dot_last(window(vhal, b, g), grad_stack)
            probs = ehal[it].astype(f32) * inv_hal[pl.ds(it, 1), :]
            grad_score = (probs * (grad_prob - middle_row)).astype(bf16)
            wide = wide + dot(window_t(kthal, b, g), grad_score)
            dq[g, pl.ds(pl.multiple_of(b * BLK, BLK), BLK), :] = (
                (diagonal(wide) * HEAD_DIM ** (-0.5)).T.astype(bf16)
            )
        return carry

    lax.fori_loop(0, OWN, backward, 0, unroll=True)

    grads.wait_recv()

    for side in range(2):
        for b in range(OWN):
            for g in range(NGRP):
                put_stack(
                    domr,
                    (side * OWN + b) * NGRP + g,
                    dor[side, b * BLK : (b + 1) * BLK, g * SLAB : (g + 1) * SLAB].astype(f32),
                )
    middles.wait_recv()

    for side, b, first, last, begin in pairs:

        def remote(g, carry, side=side, b=b, first=first, last=last, begin=begin):
            it = b * NGRP + g
            grad_stack = domr[side * NIT + it]
            own = slice(first * BLK, last * BLK)
            probs = prem[side, g, begin : begin + (last - first) * BLK, :]
            grad_prob = dot_last(vown[g, own, :], grad_stack)
            grad_score = probs.astype(f32) * (grad_prob - centrer[side, pl.ds(it, 1), :])
            dk[g, own, :] += dot(grad_score.astype(bf16), qmr[side * NIT + it])
            dv[g, own, :] += dot(probs, grad_stack)
            return carry

        lax.fori_loop(0, NGRP, remote, 0, unroll=True)

    def finish(r, carry):
        part = pl.ds(pl.multiple_of(r * 256, 256), 256)
        grad = None
        for g in range(NGRP):
            cols = slice(g * SLAB, (g + 1) * SLAB)
            term = dot_last(dq[g, part, :], wq_ref[:, cols])
            term += dot_last(dk[g, part, :].astype(bf16), wk_ref[:, cols])
            term += dot_last(dv[g, part, :].astype(bf16), wv_ref[:, cols])
            grad = term if grad is None else grad + term
        normed, inverse = norm_parts(x_ref[part, :].astype(f32))
        out_ref[part, :] = (
            gmr[part, :] + norm_reverse(grad, normed, inverse, ag_ref[...])
        ).astype(out_ref.dtype)
        return carry

    lax.fori_loop(0, 2, finish, 0, unroll=True)

    for done in (
        lists,
        levels,
        middles,
        grads,
        ring_up,
        ring_down,
        cross_up,
        cross_down,
        twin_one,
        twin_two,
        twin_three,
    ):
        done.wait_send()


def body(nodes, tensors, *args):
    (x, og, ag, fg, wq, wk, wv, wo, wu, wd, nbr, cnt, nm) = args
    rows, width = x.shape
    vm = pl.BlockSpec(memory_space=pltpu.VMEM)
    sm = pl.BlockSpec(memory_space=pltpu.SMEM)
    hbm = pl.BlockSpec(memory_space=pl.ANY)
    V = pltpu.VMEM
    own, hal = OWN * BLK, 2 * SPAN * BLK
    return pl.pallas_call(
        functools.partial(kernel, nodes, tensors),
        out_shape=jax.ShapeDtypeStruct((rows, width), bf16),
        in_specs=[hbm] * 2 + [vm] * 2 + [hbm] * 6 + [sm] * 2 + [hbm],
        out_specs=vm,
        scratch_shapes=[
            V((rows, width), bf16),
            V((rows, width), bf16),
            V((width, width), bf16),
            V((width, width), bf16),
            V((width, width), bf16),
            V((width, width), bf16),
            V(nm.shape, jnp.int32),
            V((2, rows, width), bf16),
            V((2, rows, width), bf16),
            V((NIT, STK, SLAB), bf16),
            V((2 * NIT, STK, SLAB), bf16),
            V((NGRP, own, SLAB), bf16),
            V((NGRP, own, SLAB), bf16),
            V((NGRP, SLAB, own), bf16),
            V((NGRP, SLAB, own), bf16),
            V((NGRP, hal, SLAB), bf16),
            V((NGRP, hal, SLAB), bf16),
            V((NGRP, SLAB, hal), bf16),
            V((NGRP, SLAB, hal), bf16),
            V((own + hal, BLK), f32),
            pltpu.SMEM((OWN * (OWN + HWIN),), f32),
            V((2, OWN * OWN, BLK), f32),
            V((2, OWN * OWN, BLK), f32),
            V((4, 2, width, width), bf16),
            V((NGRP, HWIN * BLK, STK), f32),
            V((NIT, own, STK), bf16),
            V((NIT, HWIN * BLK, STK), bf16),
            V((NGRP, rows, SLAB), bf16),
            V((NIT, SLAB, BLK), f32),
            V((NIT, STK), f32),
            V((NIT, STK), f32),
            V((NIT, STK), f32),
            V((2, NIT, STK), f32),
            V((NIT, STK), f32),
            V((2, NIT, STK), f32),
            V((NIT, STK), f32),
            V((NIT, STK), f32),
            V((rows, width), f32),
            V((rows, width), bf16),
            V((rows, width), f32),
            V((rows, width), f32),
            V((rows, width), bf16),
            V((2, rows, width), bf16),
            V((NIT, STK, SLAB), bf16),
            V((2 * NIT, STK, SLAB), bf16),
            V((2, NGRP, OWN * (OWN + 1) // 2 * BLK, STK), bf16),
            V((NGRP, rows, SLAB), bf16),
            V((NGRP, rows, SLAB), f32),
            V((NGRP, rows, SLAB), f32),
            pltpu.SemaphoreType.DMA((17,)),
            pltpu.SemaphoreType.DMA((17,)),
            pltpu.SemaphoreType.DMA((9,)),
        ],
        compiler_params=pltpu.CompilerParams(
            collective_id=0, has_side_effects=True, vmem_limit_bytes=62 * 1024 * 1024
        ),
    )(x, og, ag.reshape(1, width), fg.reshape(1, width), wq, wk, wv, wo, wu, wd, nbr, cnt, nm)


def solution(mesh):
    return jax.shard_map(
        functools.partial(body, mesh.shape["node"], mesh.shape["tensor"]),
        mesh=mesh,
        in_specs=(
            P(("member", "node", "tensor"), None),
            P(("member", "node", "tensor"), None),
            P(),
            P(),
            P(),
            P(),
            P(),
            P(),
            P(None, "tensor"),
            P("tensor", None),
            P(("node", "tensor"), None),
            P(("node", "tensor")),
            P(),
        ),
        out_specs=P(("member", "node", "tensor"), None),
        check_vma=False,
    )
```

time: 84.4 us -> 69.1 us (0.82)
  the two profiles are of different devices: /device:TPU:1 before, /device:TPU:160 now
where the time goes in v2:
time: 69.1 us; the launch traced here: 68.6 us
  Pallas kernels  66.7 us (97%)
  local copies, waits for them, and re-layouts  1.87 us (3%)
    pallas_call x1, Pallas kernels, body(): pl.pallas_call(functools.partial(kernel, nodes, tensors), out_shape=jax.S...  66.7 us
    unnamed x1, local copies, waits for them, and re-layouts  1.87 us

profile of v2, /device:TPU:160, one launch (start us, length us, event | category | flops | bytes accessed | tf_op | source)
XLA Modules:
  0.0 68.6 jit_solution(8944502199414426262)
XLA Ops:
  0.0 66.7 %shard_map.127 = bf16[512,512]{1,0:T(8,128)(2,1)} custom-call(bf16[512,512]{1,0:T(8,128)(2,1)} %x_hbm.1, bf16[512,512]{1,0:T(8,128)(2,1)} %og_hbm.1, f32[1,512]{1,0:T(1,128)} %bitcast.2, f32[1,512]{1,0:T(1,128)} %bitcast.3, bf16[512,512]{1,0:T(8,128)(2,1)} %wq_hbm.1, bf16[512,512]{1,0:T(8,128)(2,1)} %wk_hbm.1, bf16[512,512]{1,0:T(8,128)(2,1)} %wv_hbm.1, ...), custom_call_target="tpu_custom_call" | custom-call | tf_op jit(solution)/shard_map/pallas_call | solution.py:645
  66.7 1.9 %copy.15 = bf16[512,512]{1,0:T(8,128)(2,1)} copy(bf16[512,512]{1,0:T(8,128)(2,1)} %shard_map.127) | data formatting | bytes 1048576

commit v3 on v2

--- a/solution.py
+++ b/solution.py
@@ -19,6 +19,8 @@
 NGRP = HEADS // GRP
 STK = GRP * BLK
 NIT = OWN * NGRP
+RING = 4
+QUART = 128
 
 NORM_EPS = 1e-05
 GELU_C = 0.7978845608028654
@@ -164,17 +166,21 @@
     up = (member, node, lax.rem(tensor + 1, tensors))
     down = (member, node, lax.rem(tensor + tensors - 1, tensors))
     twin = (1 - member, node, tensor)
+    column = lax.rem(node, RING)
+    plane = node - column
+    east = (member, plane + lax.rem(column + 1, RING), tensor)
+    west = (member, plane + lax.rem(column + RING - 1, RING), tensor)
 
     loads = {}
     for i, (name, src, dst) in enumerate(
         (
+            ("wu", wu_hbm, wbuf.at[0, 0]),
+            ("wd", wd_hbm, wbuf.at[0, 1]),
             ("x", x_hbm, x_ref),
             ("wk", wk_hbm, wk_ref),
             ("wv", wv_hbm, wv_ref),
             ("wq", wq_hbm, wq_ref),
             ("nm", nm_hbm, nm_ref),
-            ("wu", wu_hbm, wbuf.at[0, 0]),
-            ("wd", wd_hbm, wbuf.at[0, 1]),
             ("wo", wo_hbm, wo_ref),
             ("og", og_hbm, og_ref),
         )
@@ -183,7 +189,7 @@
         loads[name].start()
 
     barrier = pltpu.get_barrier_semaphore()
-    for peer in (up, down, twin):
+    for peer in (up, down, east, west, twin):
         pl.semaphore_signal(barrier, inc=1, device_id=peer, device_id_type=MESH)
 
     @pl.when(has_right)
@@ -194,7 +200,7 @@
     def _():
         pl.semaphore_signal(barrier, inc=1, device_id=left, device_id_type=MESH)
 
-    pl.semaphore_wait(barrier, 3 + has_right.astype(jnp.int32) + has_left.astype(jnp.int32))
+    pl.semaphore_wait(barrier, 5 + has_right.astype(jnp.int32) + has_left.astype(jnp.int32))
 
     def copy(slot, src, dst, peer):
         return pltpu.make_async_remote_copy(
@@ -229,8 +235,53 @@
         def wait_recv(self):
             self.each(has_left, has_right, lambda c: c.wait_recv())
 
-    rows = Pair(0, x_hbm, x_hbm, halo)
-    rows.start()
+    def quarter(turn, start=0, count=QUART):
+        place_x = lax.rem(column + turn + RING, RING)
+        return pl.ds(pl.multiple_of(place_x * QUART + start, 64), count)
+
+    def stripe(first, parts, chunk):
+        return wbuf.at[pl.ds(first, parts), member, chunk]
+
+    mine = quarter(0)
+
+    class Pull:
+        def __init__(self, slot, part, peer):
+            self.made = lambda src: copy(slot, src.at[mine], wbuf.at[part, member, mine], peer)
+
+        def start(self):
+            @pl.when(member == 0)
+            def _():
+                self.made(wu_hbm).start()
+
+            @pl.when(member == 1)
+            def _():
+                self.made(wd_hbm).start()
+
+        def wait_send(self):
+            self.made(wu_hbm).wait_send()
+
+        def wait_recv(self):
+            self.made(wu_hbm).wait_recv()
+
+    pull_up = Pull(4, 1, up)
+    pull_down = Pull(5, 2, down)
+    pull_up.start()
+    pull_down.start()
+
+    class Halves:
+        def __init__(self, slots, src, dst):
+            self.parts = [
+                Pair(slot, src.at[half], src.at[half], dst.at[:, half])
+                for slot, half in zip(slots, (pl.ds(0, 256), pl.ds(256, 256)))
+            ]
+
+        def wait_send(self):
+            for part in self.parts:
+                part.wait_send()
+
+    rows = Halves((0, 24), x_hbm, halo)
+    rows.parts[0].start()
+    rows.parts[1].start()
 
     def listed(b, wanted):
         hit = jnp.int32(0)
@@ -358,25 +409,55 @@
 
     lax.fori_loop(0, OWN, forward_own, 0, unroll=True)
 
-    loads["wu"].wait()
-    loads["wd"].wait()
-    rows.wait_send()
-    ring_up = copy(4, wbuf.at[0, member], wbuf.at[1, member], up)
-    ring_down = copy(5, wbuf.at[0, member], wbuf.at[2, member], down)
-    ring_up.start()
-    ring_down.start()
-    rows.wait_recv()
+    def hand_over(slot, first, parts, chunk):
+        made = copy(slot, stripe(first, parts, chunk), stripe(first, parts, chunk), twin)
+        made.start()
+        handed.append((made, slot, first, parts, chunk))
+
+    handed = []
+
+    pull_up.wait_recv()
+    pull_down.wait_recv()
+    half_low, half_high = quarter(0, 0, 64), quarter(0, 64, 64)
+    cross_up = copy(6, wbuf.at[1, member, half_low], wbuf.at[3, member, half_low], up)
+    cross_down = copy(7, wbuf.at[2, member, half_high], wbuf.at[3, member, half_high], down)
+    cross_up.start()
+    cross_down.start()
+    near_east = copy(8, stripe(1, 2, mine), stripe(1, 2, mine), east)
+    near_west = copy(9, stripe(1, 2, mine), stripe(1, 2, mine), west)
+    near_east.start()
+    near_west.start()
+    hand_over(20, 1, 2, mine)
+
+    cross_up.wait_recv()
+    cross_down.wait_recv()
+    far_east = copy(10, stripe(3, 1, mine), stripe(3, 1, mine), east)
+    far_west = copy(17, stripe(3, 1, mine), stripe(3, 1, mine), west)
+    far_east.start()
+    far_west.start()
+
+    near_east.wait_recv()
+    near_west.wait_recv()
+    from_west, from_east = quarter(-1, 0, 64), quarter(1, 64, 64)
+    on_east = copy(18, stripe(1, 2, from_west), stripe(1, 2, from_west), east)
+    on_west = copy(19, stripe(1, 2, from_east), stripe(1, 2, from_east), west)
+    on_east.start()
+    on_west.start()
+    hand_over(23, 1, 2, quarter(-1))
+    hand_over(26, 1, 2, quarter(1))
 
     def halo_rows(r, carry):
-        side = r // 2
-        base = pl.multiple_of(lax.rem(r, 2) * 256, 256)
+        side = lax.rem(r, 2)
+        base = pl.multiple_of((r // 2) * 256, 256)
         normed, _ = norm_parts(halo[side, pl.ds(base, 256), :].astype(f32))
         normed = (normed * ag_ref[...]).astype(bf16)
         n1h[side, pl.ds(base, 256), :] = normed
         keys_values(normed, side * SPAN * BLK + base, khal, vhal, kthal, vthal)
         return carry
 
-    lax.fori_loop(0, 4, halo_rows, 0, unroll=True)
+    for half in range(2):
+        rows.parts[half].wait_recv()
+        lax.fori_loop(2 * half, 2 * half + 2, halo_rows, 0, unroll=True)
 
     def window(ref, b, g):
         return ref[g, pl.ds(pl.multiple_of(b * BLK, BLK), HWIN * BLK), :]
@@ -410,7 +491,22 @@
             inv_hal[pl.ds(it, 1), :] = distant
         return carry
 
-    lax.fori_loop(0, OWN, forward_halo, 0, unroll=True)
+    lax.fori_loop(0, 2, forward_halo, 0, unroll=True)
+
+    far_east.wait_recv()
+    far_west.wait_recv()
+    last_east = copy(21, stripe(3, 1, from_west), stripe(3, 1, from_west), east)
+    last_west = copy(22, stripe(3, 1, from_east), stripe(3, 1, from_east), west)
+    last_east.start()
+    last_west.start()
+    on_east.wait_recv()
+    on_west.wait_recv()
+    hand_over(27, 1, 2, quarter(2))
+    hand_over(28, 3, 1, mine)
+    hand_over(29, 3, 1, quarter(-1))
+    hand_over(30, 3, 1, quarter(1))
+
+    lax.fori_loop(2, OWN, forward_halo, 0, unroll=True)
 
     levels = Pair(11, lse, lse, lser)
     levels.start()
@@ -430,6 +526,8 @@
 
     lax.fori_loop(0, 2, middle, 0, unroll=True)
     loads["og"].wait()
+    loads["wu"].wait()
+    loads["wd"].wait()
 
     def hidden(slot):
         def run(r, carry):
@@ -445,73 +543,23 @@
 
     other = 1 - member
 
-    def arrival(slot_id, slot):
-        return copy(slot_id, wbuf.at[slot, other], wbuf.at[slot, other], twin)
-
-    ring_up.wait_recv()
-    ring_down.wait_recv()
-    cross_up = copy(
-        6, wbuf.at[1, member, pl.ds(0, 256)], wbuf.at[3, member, pl.ds(0, 256)], up
-    )
-    cross_down = copy(
-        7, wbuf.at[2, member, pl.ds(256, 256)], wbuf.at[3, member, pl.ds(256, 256)], down
-    )
-    cross_up.start()
-    cross_down.start()
-    twin_one = copy(8, wbuf.at[1, member], wbuf.at[1, member], twin)
-    twin_two = copy(9, wbuf.at[2, member], wbuf.at[2, member], twin)
-    twin_one.start()
-    twin_two.start()
+    def handed_here(first):
+        for _, slot, begin, parts, chunk in handed:
+            if begin == first:
+                landed = wbuf.at[pl.ds(begin, parts), other, chunk]
+                copy(slot, landed, landed, twin).wait_recv()
 
     hidden(0)
-
-    def far_queries(r, carry):
-        side = r // 2
-        base = pl.multiple_of(lax.rem(r, 2) * 256, 256)
-        queries(n1h[side, pl.ds(base, 256), :], qmr, r * 2 * NGRP)
-        return carry
-
-    lax.fori_loop(0, 4, far_queries, 0, unroll=True)
-    arrival(8, 1).wait_recv()
+    last_east.wait_recv()
+    last_west.wait_recv()
+    hand_over(31, 3, 1, quarter(2))
+    handed_here(1)
     hidden(1)
-    arrival(9, 2).wait_recv()
     hidden(2)
-
-    pairs = []
-    for side in range(2):
-        begin = 0
-        for b in range(OWN):
-            first, last = (0, b + 1) if side == 0 else (b, OWN)
-            pairs.append((side, b, first, last, begin * BLK))
-            begin += last - first
-
-    lists.wait_recv()
-    levels.wait_recv()
-    for side, b, first, last, begin in pairs:
-
-        def remote_probs(g, carry, side=side, b=b, first=first, last=last, begin=begin):
-            it = b * NGRP + g
-            level = lser[side, pl.ds(it, 1), :]
-            s = dot_last(kown[g, first * BLK : last * BLK, :], qmr[side * NIT + it])
-            for c in range(first, last):
-                at = (c - first) * BLK
-                row = b * OWN + c
-                shift = lanes4(vbr[side, row : row + 1, :]) - level
-                bias = lanes4(live[c * BLK : (c + 1) * BLK, :]) + shift
-                prem[side, g, begin + at : begin + at + BLK, :] = jnp.exp(
-                    s[at : at + BLK, :] + bias
-                ).astype(bf16)
-            return carry
-
-        lax.fori_loop(0, NGRP, remote_probs, 0, unroll=True)
-
-    cross_up.wait_recv()
-    cross_down.wait_recv()
-    twin_three = copy(10, wbuf.at[3, member], wbuf.at[3, member], twin)
-    twin_three.start()
-    arrival(10, 3).wait_recv()
+    handed_here(3)
     hidden(3)
 
+    grads = Halves((13, 32), dob, dor)
     for r in range(2):
         part = slice(r * 256, (r + 1) * 256)
         up_grad = og_ref[part, :].astype(f32)
@@ -521,9 +569,7 @@
         res_bf = res.astype(bf16)
         n2[part, :] = res_bf
         dob[part, :] = dot_last(res_bf, wo_ref[...]).astype(bf16)
-
-    grads = Pair(13, dob, dob, dor)
-    grads.start()
+        grads.parts[r].start()
 
     for r in range(2):
         part = slice(r * 256, (r + 1) * 256)
@@ -574,32 +620,61 @@
 
     lax.fori_loop(0, OWN, backward, 0, unroll=True)
 
-    grads.wait_recv()
-
+    def far_queries(r, carry):
+        side = r // 2
+        base = pl.multiple_of(lax.rem(r, 2) * 256, 256)
+        queries(n1h[side, pl.ds(base, 256), :], qmr, r * 2 * NGRP)
+        return carry
+
+    lax.fori_loop(0, 4, far_queries, 0, unroll=True)
+    pairs = []
     for side in range(2):
+        begin = 0
         for b in range(OWN):
+            first, last = (0, b + 1) if side == 0 else (b, OWN)
+            pairs.append((side, b, first, last, begin * BLK))
+            begin += last - first
+    pairs.sort(key=lambda pair: pair[1])
+
+    lists.wait_recv()
+    levels.wait_recv()
+    for side, b, first, last, begin in pairs:
+
+        def remote_probs(g, carry, side=side, b=b, first=first, last=last, begin=begin):
+            it = b * NGRP + g
+            level = lser[side, pl.ds(it, 1), :]
+            s = dot_last(kown[g, first * BLK : last * BLK, :], qmr[side * NIT + it])
+            for c in range(first, last):
+                at = (c - first) * BLK
+                row = b * OWN + c
+                shift = lanes4(vbr[side, row : row + 1, :]) - level
+                bias = lanes4(live[c * BLK : (c + 1) * BLK, :]) + shift
+                prem[side, g, begin + at : begin + at + BLK, :] = jnp.exp(
+                    s[at : at + BLK, :] + bias
+                ).astype(bf16)
+            return carry
+
+        lax.fori_loop(0, NGRP, remote_probs, 0, unroll=True)
+
+    middles.wait_recv()
+    for half in range(2):
+        grads.parts[half].wait_recv()
+        for side, b, first, last, begin in pairs[half * OWN : (half + 1) * OWN]:
             for g in range(NGRP):
+                it = side * NIT + b * NGRP + g
                 put_stack(
                     domr,
-                    (side * OWN + b) * NGRP + g,
+                    it,
                     dor[side, b * BLK : (b + 1) * BLK, g * SLAB : (g + 1) * SLAB].astype(f32),
                 )
-    middles.wait_recv()
-
-    for side, b, first, last, begin in pairs:
-
-        def remote(g, carry, side=side, b=b, first=first, last=last, begin=begin):
-            it = b * NGRP + g
-            grad_stack = domr[side * NIT + it]
-            own = slice(first * BLK, last * BLK)
-            probs = prem[side, g, begin : begin + (last - first) * BLK, :]
-            grad_prob = dot_last(vown[g, own, :], grad_stack)
-            grad_score = probs.astype(f32) * (grad_prob - centrer[side, pl.ds(it, 1), :])
-            dk[g, own, :] += dot(grad_score.astype(bf16), qmr[side * NIT + it])
-            dv[g, own, :] += dot(probs, grad_stack)
-            return carry
-
-        lax.fori_loop(0, NGRP, remote, 0, unroll=True)
+                grad_stack = domr[it]
+                own = slice(first * BLK, last * BLK)
+                probs = prem[side, g, begin : begin + (last - first) * BLK, :]
+                grad_prob = dot_last(vown[g, own, :], grad_stack)
+                middle_row = centrer[side, b * NGRP + g : b * NGRP + g + 1, :]
+                grad_score = (probs.astype(f32) * (grad_prob - middle_row)).astype(bf16)
+                dk[g, own, :] += dot(grad_score, qmr[it])
+                dv[g, own, :] += dot(probs, grad_stack)
 
     def finish(r, carry):
         part = pl.ds(pl.multiple_of(r * 256, 256), 256)
@@ -619,17 +694,24 @@
     lax.fori_loop(0, 2, finish, 0, unroll=True)
 
     for done in (
+        rows,
         lists,
         levels,
         middles,
         grads,
-        ring_up,
-        ring_down,
+        pull_up,
+        pull_down,
         cross_up,
         cross_down,
-        twin_one,
-        twin_two,
-        twin_three,
+        near_east,
+        near_west,
+        far_east,
+        far_west,
+        on_east,
+        on_west,
+        last_east,
+        last_west,
+        *[made for made, *_ in handed],
     ):
         done.wait_send()
 
@@ -697,8 +779,8 @@
             V((NGRP, rows, SLAB), bf16),
             V((NGRP, rows, SLAB), f32),
             V((NGRP, rows, SLAB), f32),
-            pltpu.SemaphoreType.DMA((17,)),
-            pltpu.SemaphoreType.DMA((17,)),
+            pltpu.SemaphoreType.DMA((34,)),
+            pltpu.SemaphoreType.DMA((34,)),
             pltpu.SemaphoreType.DMA((9,)),
         ],
         compiler_params=pltpu.CompilerParams(

time: 69.1 us -> 69.1 us (level)
  no operation moved by 1% of the time
where the time goes in v3:
time: 69.1 us; the launch traced here: 69 us
  Pallas kernels  67.1 us (97%)
  local copies, waits for them, and re-layouts  1.87 us (3%)
    pallas_call x1, Pallas kernels, body(): pl.pallas_call(functools.partial(kernel, nodes, tensors), out_shape=jax.S...  67.1 us
    unnamed x1, local copies, waits for them, and re-layouts  1.87 us

profile of v3, /device:TPU:160, one launch (start us, length us, event | category | flops | bytes accessed | tf_op | source)
XLA Modules:
  0.0 69.0 jit_solution(6518587262945040429)
XLA Ops:
  0.0 67.1 %shard_map.127 = bf16[512,512]{1,0:T(8,128)(2,1)} custom-call(bf16[512,512]{1,0:T(8,128)(2,1)} %x_hbm.1, bf16[512,512]{1,0:T(8,128)(2,1)} %og_hbm.1, f32[1,512]{1,0:T(1,128)} %bitcast.2, f32[1,512]{1,0:T(1,128)} %bitcast.3, bf16[512,512]{1,0:T(8,128)(2,1)} %wq_hbm.1, bf16[512,512]{1,0:T(8,128)(2,1)} %wk_hbm.1, bf16[512,512]{1,0:T(8,128)(2,1)} %wv_hbm.1, ...), custom_call_target="tpu_custom_call" | custom-call | tf_op jit(solution)/shard_map/pallas_call | solution.py:727
  67.1 1.9 %copy.15 = bf16[512,512]{1,0:T(8,128)(2,1)} copy(bf16[512,512]{1,0:T(8,128)(2,1)} %shard_map.127) | data formatting | bytes 1048576

commit v4 on v3

--- a/solution.py
+++ b/solution.py
@@ -281,7 +281,6 @@
 
     rows = Halves((0, 24), x_hbm, halo)
     rows.parts[0].start()
-    rows.parts[1].start()
 
     def listed(b, wanted):
         hit = jnp.int32(0)
@@ -362,6 +361,7 @@
         return carry
 
     lax.fori_loop(0, 2, own_rows, 0, unroll=True)
+    rows.parts[1].start()
 
     loads["nm"].wait()
     for i in range(OWN + 2 * SPAN):
@@ -429,6 +429,19 @@
     near_west.start()
     hand_over(20, 1, 2, mine)
 
+    def halo_rows(r, carry):
+        side = lax.rem(r, 2)
+        base = pl.multiple_of((r // 2) * 256, 256)
+        normed, _ = norm_parts(halo[side, pl.ds(base, 256), :].astype(f32))
+        normed = (normed * ag_ref[...]).astype(bf16)
+        n1h[side, pl.ds(base, 256), :] = normed
+        keys_values(normed, side * SPAN * BLK + base, khal, vhal, kthal, vthal)
+        return carry
+
+    for half in range(2):
+        rows.parts[half].wait_recv()
+        lax.fori_loop(2 * half, 2 * half + 2, halo_rows, 0, unroll=True)
+
     cross_up.wait_recv()
     cross_down.wait_recv()
     far_east = copy(10, stripe(3, 1, mine), stripe(3, 1, mine), east)
@@ -445,19 +458,6 @@
     on_west.start()
     hand_over(23, 1, 2, quarter(-1))
     hand_over(26, 1, 2, quarter(1))
-
-    def halo_rows(r, carry):
-        side = lax.rem(r, 2)
-        base = pl.multiple_of((r // 2) * 256, 256)
-        normed, _ = norm_parts(halo[side, pl.ds(base, 256), :].astype(f32))
-        normed = (normed * ag_ref[...]).astype(bf16)
-        n1h[side, pl.ds(base, 256), :] = normed
-        keys_values(normed, side * SPAN * BLK + base, khal, vhal, kthal, vthal)
-        return carry
-
-    for half in range(2):
-        rows.parts[half].wait_recv()
-        lax.fori_loop(2 * half, 2 * half + 2, halo_rows, 0, unroll=True)
 
     def window(ref, b, g):
         return ref[g, pl.ds(pl.multiple_of(b * BLK, BLK), HWIN * BLK), :]
@@ -491,7 +491,10 @@
             inv_hal[pl.ds(it, 1), :] = distant
         return carry
 
-    lax.fori_loop(0, 2, forward_halo, 0, unroll=True)
+    lax.fori_loop(0, OWN, forward_halo, 0, unroll=True)
+
+    levels = Pair(11, lse, lse, lser)
+    levels.start()
 
     far_east.wait_recv()
     far_west.wait_recv()
@@ -506,11 +509,6 @@
     hand_over(29, 3, 1, quarter(-1))
     hand_over(30, 3, 1, quarter(1))
 
-    lax.fori_loop(2, OWN, forward_halo, 0, unroll=True)
-
-    levels = Pair(11, lse, lse, lser)
-    levels.start()
-
     loads["wo"].wait()
 
     def middle(r, carry):
@@ -556,6 +554,14 @@
     handed_here(1)
     hidden(1)
     hidden(2)
+
+    def far_queries(r, carry):
+        side = r // 2
+        base = pl.multiple_of(lax.rem(r, 2) * 256, 256)
+        queries(n1h[side, pl.ds(base, 256), :], qmr, r * 2 * NGRP)
+        return carry
+
+    lax.fori_loop(0, 4, far_queries, 0, unroll=True)
     handed_here(3)
     hidden(3)
 
@@ -620,13 +626,6 @@
 
     lax.fori_loop(0, OWN, backward, 0, unroll=True)
 
-    def far_queries(r, carry):
-        side = r // 2
-        base = pl.multiple_of(lax.rem(r, 2) * 256, 256)
-        queries(n1h[side, pl.ds(base, 256), :], qmr, r * 2 * NGRP)
-        return carry
-
-    lax.fori_loop(0, 4, far_queries, 0, unroll=True)
     pairs = []
     for side in range(2):
         begin = 0

time: 69.1 us -> 67.6 us (0.978)
  Pallas kernels: 67.1 us -> 65.5 us
    pallas_call x1, Pallas kernels: 67.1 us -> 65.5 us  [body(): pl.pallas_call(functools.partial(kernel, nodes, tensors), out_shape=jax.S...]
where the time goes in v4:
time: 67.6 us; the launch traced here: 67.4 us
  Pallas kernels  65.5 us (97%)
  local copies, waits for them, and re-layouts  1.87 us (3%)
    pallas_call x1, Pallas kernels, body(): pl.pallas_call(functools.partial(kernel, nodes, tensors), out_shape=jax.S...  65.5 us
    unnamed x1, local copies, waits for them, and re-layouts  1.87 us

profile of v4, /device:TPU:160, one launch (start us, length us, event | category | flops | bytes accessed | tf_op | source)
XLA Modules:
  0.0 67.4 jit_solution(11326589590558631116)
XLA Ops:
  0.0 65.5 %shard_map.127 = bf16[512,512]{1,0:T(8,128)(2,1)} custom-call(bf16[512,512]{1,0:T(8,128)(2,1)} %x_hbm.1, bf16[512,512]{1,0:T(8,128)(2,1)} %og_hbm.1, f32[1,512]{1,0:T(1,128)} %bitcast.2, f32[1,512]{1,0:T(1,128)} %bitcast.3, bf16[512,512]{1,0:T(8,128)(2,1)} %wq_hbm.1, bf16[512,512]{1,0:T(8,128)(2,1)} %wk_hbm.1, bf16[512,512]{1,0:T(8,128)(2,1)} %wv_hbm.1, ...), custom_call_target="tpu_custom_call" | custom-call | tf_op jit(solution)/shard_map/pallas_call | solution.py:726
  65.5 1.9 %copy.15 = bf16[512,512]{1,0:T(8,128)(2,1)} copy(bf16[512,512]{1,0:T(8,128)(2,1)} %shard_map.127) | data formatting | bytes 1048576

commit v5 on v4

--- a/solution.py
+++ b/solution.py
@@ -548,12 +548,13 @@
                 copy(slot, landed, landed, twin).wait_recv()
 
     hidden(0)
+    handed_here(1)
+    hidden(1)
+    hidden(2)
+
     last_east.wait_recv()
     last_west.wait_recv()
     hand_over(31, 3, 1, quarter(2))
-    handed_here(1)
-    hidden(1)
-    hidden(2)
 
     def far_queries(r, carry):
         side = r // 2

time: 67.6 us -> 68.6 us (1.015)
  Pallas kernels: 65.5 us -> 66.5 us
    pallas_call x1, Pallas kernels: 65.5 us -> 66.5 us  [body(): pl.pallas_call(functools.partial(kernel, nodes, tensors), out_shape=jax.S...]
where the time goes in v5:
time: 68.6 us; the launch traced here: 68.3 us
  Pallas kernels  66.5 us (97%)
  local copies, waits for them, and re-layouts  1.87 us (3%)
    pallas_call x1, Pallas kernels, body(): pl.pallas_call(functools.partial(kernel, nodes, tensors), out_shape=jax.S...  66.5 us
    unnamed x1, local copies, waits for them, and re-layouts  1.87 us

profile of v5, /device:TPU:160, one launch (start us, length us, event | category | flops | bytes accessed | tf_op | source)
XLA Modules:
  0.0 68.3 jit_solution(4368435649917025737)
XLA Ops:
  0.0 66.5 %shard_map.127 = bf16[512,512]{1,0:T(8,128)(2,1)} custom-call(bf16[512,512]{1,0:T(8,128)(2,1)} %x_hbm.1, bf16[512,512]{1,0:T(8,128)(2,1)} %og_hbm.1, f32[1,512]{1,0:T(1,128)} %bitcast.2, f32[1,512]{1,0:T(1,128)} %bitcast.3, bf16[512,512]{1,0:T(8,128)(2,1)} %wq_hbm.1, bf16[512,512]{1,0:T(8,128)(2,1)} %wk_hbm.1, bf16[512,512]{1,0:T(8,128)(2,1)} %wv_hbm.1, ...), custom_call_target="tpu_custom_call" | custom-call | tf_op jit(solution)/shard_map/pallas_call | solution.py:727
  66.5 1.9 %copy.15 = bf16[512,512]{1,0:T(8,128)(2,1)} copy(bf16[512,512]{1,0:T(8,128)(2,1)} %shard_map.127) | data formatting | bytes 1048576
